TPU v7x, 256 devices: a whole 4x4x8 slice. The times are simulated.
256 devices in a mesh: space: 16 (over y, z_lo, core), tm: 16 (over x, z_hi).
Axes of the slice: x: 4, y: 4, z: 8 (z_hi: 4, z_lo: 2; z = z_hi * 2 + z_lo), core: 2. Of those that a mesh axis runs over, the one named last changes fastest.
Arguments:
- probe_field: bfloat16 [16384, 4096], P('space', 'tm'), may hold values from -5 to 5
- kappa: float32 [16384], P('space'), may hold values from 0.1 to 1
- theta_space: float32 [64], P('tm'), may hold values from 0.3 to 1
- theta_time: float32 [64], P('tm'), may hold values from 0.2 to 0.8
- diag_blocks: bfloat16 [128, 128, 128], P('space'), may hold values from -0.05 to 1.05
- off_blocks: bfloat16 [128, 8, 128, 128], P('space'), may hold values from -0.375 to 0.375
- block_cols: int32 [128, 8], P('space'), may hold values from 0 to 11
- halo_needs: int32 [64], P('space'), may hold values from 0 to 7
- covariates: bfloat16 [524288, 256], P(('space', 'tm')), may hold values from -4 to 4
- obs_owner: int32 [524288, 1], P(('space', 'tm')), may hold values from 0 to 15; in each aligned block of 2048 rows (0 to 2047, 2048 to 4095, ...) at most 256 rows name the same one
- obs_cell: int32 [524288], P(('space', 'tm')), may hold values from 0 to 4095
- svc_coef: bfloat16 [16384, 256], P('space'), may hold values from -0.375 to 0.375
Outputs:
- solution: float32 [16384, 4096], P('space', 'tm')
- grads: float32 [2, 4096], P(None, 'tm')
Inputs may be any that keep to these rules, and one draw needn't show every extreme that they name: `obs_owner`: in each aligned block of 2048 rows (the rows of one device) no owner is named by more than 256 rows, a bound that some block reaches.
All inputs are finite; a program needn't handle non-finite values.
Results may differ from a plain program's by a relative error of at most 0.0021.
Values may be sent and summed in bfloat16 or wider, within the bound.
A program may use at most 64 MiB of HBM per device.

v0:
```python
import jax
import jax.numpy as jnp
from jax import lax
from jax.sharding import PartitionSpec as P

NB_DEV = 8
BLOCK = 128
HALO_B = 2
T_DEV = 4
PROBES = 64
NCOV = 256
OBS_DEV = 2048
ITERS = 4
NODES_DEV = 1024


relaxation = 0.6


def with_halo(array, sides, width):
    for axis, dim in sides:
        peers, length = (lax.axis_size(axis), array.shape[dim])
        up = [(i, (i + 1) % peers) for i in range(peers - 1)]
        down = [(j, i) for i, j in up]
        last = lax.slice_in_dim(array, length - width, length, axis=dim)
        initial = lax.slice_in_dim(array, 0, width, axis=dim)
        before = lax.ppermute(last, axis, up)
        after = lax.ppermute(initial, axis, down)
        array = jnp.concatenate([before, array, after], axis=dim)
    return array


def shards(
    probe_field,
    kappa,
    theta_space,
    theta_time,
    diag_blocks,
    off_blocks,
    block_cols,
    halo_needs,
    covariates,
    obs_owner,
    obs_cell,
    svc_coef,
):
    space_count = lax.axis_size("space")
    columns = probe_field.shape[1]
    width_local = NB_DEV + 2 * HALO_B
    probe_vals = probe_field.astype(jnp.float32)
    sdiag = jnp.diagonal(diag_blocks, axis1=1, axis2=2).astype(jnp.float32).reshape(NODES_DEV)
    scale_space = jnp.repeat(theta_space, PROBES)[None, :]
    scale_time = jnp.repeat(theta_time, PROBES)[None, :]
    base_diag = scale_space * sdiag[:, None] + 2.0 * scale_time + kappa[:, None]
    local_ids = jnp.arange(width_local, dtype=jnp.int32)
    picks = (block_cols[:, :, None] == local_ids[None, None, :]).astype(jnp.float32)
    own_pick = (jnp.arange(NB_DEV, dtype=jnp.int32)[:, None] == local_ids[None, :]).astype(
        jnp.float32
    )
    combined = jnp.einsum("bkm,bkij->bimj", picks, off_blocks.astype(jnp.float32))
    combined = combined + jnp.einsum("bm,bij->bimj", own_pick, diag_blocks.astype(jnp.float32))
    combined = combined.astype(jnp.bfloat16).reshape(NODES_DEV, width_local * BLOCK)
    own_part = combined[:, :NODES_DEV]
    lower_part = combined[:, NODES_DEV : NODES_DEV + HALO_B * BLOCK]
    upper_part = combined[:, NODES_DEV + HALO_B * BLOCK :]

    def spatial(field):
        arrived = with_halo(field, (("space", 0),), NODES_DEV)
        lower = (
            arrived[:NODES_DEV]
            .reshape(NB_DEV, BLOCK, columns)[halo_needs[:HALO_B]]
            .reshape(HALO_B * BLOCK, columns)
        )
        upper = (
            arrived[2 * NODES_DEV :]
            .reshape(NB_DEV, BLOCK, columns)[halo_needs[HALO_B:]]
            .reshape(HALO_B * BLOCK, columns)
        )
        total = jnp.dot(own_part, field, preferred_element_type=jnp.float32)
        total = total + jnp.dot(lower_part, lower, preferred_element_type=jnp.float32)
        total = total + jnp.dot(upper_part, upper, preferred_element_type=jnp.float32)
        return total

    def temporal(field):
        arrived = with_halo(field, (("tm", 1),), PROBES)
        return (
            2.0 * field.astype(jnp.float32)
            - arrived[:, :columns].astype(jnp.float32)
            - arrived[:, 2 * PROBES :].astype(jnp.float32)
        )

    solution = relaxation * probe_vals / base_diag
    rounded = lax.optimization_barrier(solution.astype(jnp.bfloat16))
    first_space = spatial(rounded)
    first_time = temporal(rounded)
    capacity = 2 * OBS_DEV // space_count
    owner = obs_owner[:, 0]
    hits = (owner[:, None] == jnp.arange(space_count, dtype=jnp.int32)[None, :]).astype(jnp.int32)
    earlier = jnp.cumsum(hits, axis=0) - hits
    rank = jnp.sum(earlier * hits, axis=1)
    slot = owner * capacity + rank
    send_rows = jnp.zeros((space_count * capacity, NCOV), jnp.bfloat16).at[slot].set(covariates)
    send_cells = jnp.full((space_count * capacity,), -1, jnp.int32).at[slot].set(obs_cell)
    recv_rows, recv_cells = (
        lax.all_to_all(send_rows, "space", split_axis=0, concat_axis=0, tiled=True),
        lax.all_to_all(send_cells, "space", split_axis=0, concat_axis=0, tiled=True),
    )
    live = recv_cells >= 0
    cell_ids = jnp.where(live, recv_cells, 0)
    coef_rows = svc_coef[cell_ids // T_DEV]
    eta = jnp.einsum("rc,rc->r", recv_rows, coef_rows, preferred_element_type=jnp.float32)
    obs_weight = jnp.where(live, jnp.exp(eta), 0.0)
    counted = jax.ops.segment_sum(obs_weight, cell_ids, num_segments=NODES_DEV * T_DEV)
    obs_diag = jnp.repeat(counted.reshape(NODES_DEV, T_DEV), PROBES, axis=1)
    full_diag = base_diag + obs_diag
    local_diag = kappa[:, None] + obs_diag
    applied = (
        scale_space * first_space
        + scale_time * first_time
        + local_diag * rounded.astype(jnp.float32)
    )
    solution = solution + relaxation * (probe_vals - applied) / full_diag
    for sweep in range(ITERS - 1):
        rounded = lax.optimization_barrier(solution.astype(jnp.bfloat16))
        applied = (
            scale_space * spatial(rounded)
            + scale_time * temporal(rounded)
            + local_diag * rounded.astype(jnp.float32)
        )
        solution = solution + relaxation * (probe_vals - applied) / full_diag
    rounded = solution.astype(jnp.bfloat16)
    partial_sums = jnp.stack(
        [
            jnp.sum(probe_vals * spatial(rounded), axis=0),
            jnp.sum(probe_vals * temporal(rounded), axis=0),
        ]
    )
    totals = lax.psum(partial_sums, "space")
    grads = totals / (NODES_DEV * space_count)
    return (solution, grads)


def solution(mesh):
    return jax.shard_map(
        shards,
        mesh=mesh,
        in_specs=(
            P("space", "tm"),
            P("space"),
            P("tm"),
            P("tm"),
            P("space", None, None),
            P("space", None, None, None),
            P("space", None),
            P("space"),
            P(("space", "tm"), None),
            P(("space", "tm"), None),
            P(("space", "tm")),
            P("space", None),
        ),
        out_specs=(P("space", "tm"), P(None, "tm")),
        check_vma=False,
    )
```

profile of v0, /device:TPU:5, one launch (start us, length us, event | category | flops | bytes accessed | tf_op | source)
XLA Modules:
  0.0 290.1 jit_solution(17401876110952312605)
XLA Ops:
  1.5 4.5 %reduce-window.6 = s32[16,16,128]{2,1,0:T(8,128)S(1)} reduce-window(s32[16,16,128]{2,1,0:T(8,128)S(1)} %fusion.71, s32[]{:T(128)} %constant.17.clone.1), window={size=1x1x128 pad=0_0x0_0x127_0}, to_apply=%region_0.1 | reduce-window | flops 4161536 | bytes 262148 | tf_op jit(solution)/shard_map/reduce-window
  8.3 8.8 %scatter_custom_fusion = s32[4096]{0:T(1024)} fusion(s32[2048]{0:T(1024)S(1)} %bitcast.143, s32[2048]{0:T(1024)} %param.22, s32[]{:T(128)} %constant.23.clone.1), kind=kCustom, calls=%fused_computation.143 | custom fusion | bytes 16896 | tf_op jit(solution)/shard_map/scatter | solution.py:103
  17.0 6.5 %all-to-all-start = ((s32[16,256,1]{1,2,0:T(1,128)}), s32[16,256,1]{1,2,0:T(1,128)S(1)}, u32[]{:S(2)}, u32[]{:S(2)}) async-start(s32[16,256,1]{1,2,0:T(1,128)} %bitcast.15), calls=%async_computation | async-start | bytes 32768 | tf_op jit(solution)/shard_map/all_to_all | solution.py:106
  23.6 11.3 %scatter_custom_fusion.1 = bf16[4096,256]{1,0:T(8,128)(2,1)} fusion(s32[2048]{0:T(1024)S(1)} %bitcast.144, bf16[2048,256]{1,0:T(8,128)(2,1)} %param.20, bf16[]{:T(256)} %constant.45.clone.1), kind=kCustom, calls=%fused_computation.96 | custom fusion | bytes 2097664 | tf_op jit(solution)/shard_map/scatter | solution.py:102
  34.9 5.9 %all-to-all-start.1 = ((bf16[16,256,256]{2,1,0:T(8,128)(2,1)}), bf16[16,256,256]{2,1,0:T(8,128)(2,1)}, u32[]{:S(2)}, u32[]{:S(2)}) async-start(bf16[16,256,256]{2,1,0:T(8,128)(2,1)} %bitcast.111), calls=%async_computation.1 | async-start | bytes 4194304 | tf_op jit(solution)/shard_map/all_to_all | solution.py:105
  41.3 3.1 %copy.42 = bf16[8,128,128]{0,2,1:T(8,128)(2,1)} copy(bf16[8,128,128]{2,1,0:T(8,128)(2,1)S(1)} %copy-done.7) | data formatting | bytes 524288 | tf_op args[4]
  49.7 3.5 %collective-permute-start = (bf16[1024,256]{0,1:T(8,128)(2,1)}, bf16[1024,256]{0,1:T(8,128)(2,1)}, u32[]{:S(2)}, u32[]{:S(2)}) collective-permute-start(bf16[1024,256]{0,1:T(8,128)(2,1)} %fusion.57), channel_id=1, source_target_pairs={{0,16},{16,32},{32,48},{48,64},{64,80},{80,96},{96,112},{112,128},... | collective-permute-start | bytes 1572872 | tf_op jit(solution)/shard_map/ppermute | solution.py:27
  54.9 4.9 %collective-permute-start.2 = (bf16[1024,64]{0,1:T(8,128)(2,1)}, bf16[1024,64]{0,1:T(8,128)(2,1)}, u32[]{:S(2)}, u32[]{:S(2)}) collective-permute-start(bf16[1024,64]{0,1:T(8,128)(2,1)} %get-tuple-element.16), channel_id=1, source_target_pairs={{0,1},{1,2},{2,3},{3,4},{4,5},{5,6},{6,7},{7,8},{8,9},{9,10},{10,1... | collective-permute-start | bytes 393224 | tf_op jit(solution)/shard_map/ppermute | solution.py:27
  59.8 4.2 %collective-permute-start.3 = (bf16[1024,64]{0,1:T(8,128)(2,1)}, bf16[1024,64]{0,1:T(8,128)(2,1)}, u32[]{:S(2)}, u32[]{:S(2)}) collective-permute-start(bf16[1024,64]{0,1:T(8,128)(2,1)} %get-tuple-element.17), channel_id=1, source_target_pairs={{1,0},{2,1},{3,2},{4,3},{5,4},{6,5},{7,6},{8,7},{9,8},{10,9},{11,1... | collective-permute-start | bytes 393224 | tf_op jit(solution)/shard_map/ppermute | solution.py:28
  69.6 2.8 fusion.37
  72.6 17.0 %gather_fusion.3 = bf16[4096,256]{1,0:T(8,128)(2,1)} fusion(bf16[1024,256]{1,0:T(8,128)(2,1)S(1)} %copy-done.1, s32[4096]{0:T(1024)S(1)} %broadcast_clamp_fusion), kind=kCustom, calls=%fused_computation.3 | custom fusion | bytes 4210688 | tf_op jit(solution)/shard_map/gather | solution.py:110
  95.9 2.9 fusion
  98.8 27.0 %scatter_custom_fusion.2 = f32[4096]{0:T(1024)S(1)} fusion(s32[4096]{0:T(1024)S(1)} %bitcast.142, f32[4096]{0:T(1024)S(1)} %exponential_select_fusion, f32[]{:T(128)} %constant.21.clone.1), kind=kCustom, calls=%fused_computation.145 | custom fusion | flops 4096 | bytes 16388 | tf_op jit(solution)/shard_map/scatter-add | solution.py:113
  128.0 4.2 %fusion.85 = (bf16[1024,256]{0,1:T(8,128)(2,1)S(1)}, f32[1024,256]{0,1:T(8,128)}) fusion(f32[1024,256]{0,1:T(8,128)S(1)} %get-tuple-element.19, f32[1024,256]{0,1:T(8,128)S(1)} %get-tuple-element.18, bf16[1024,64]{0,1:T(8,128)(2,1)} %collective-permute-done.3, bf16[1024,256]{0,1:T(8,128)(2,1)} %fusion.57, bf16[1024,64]{0,1:T(8,128)(2,1)} %collective-permute-done.2, ...), kind=kOutput, calls=%fused_computation.162 | convolution fusion | flops 141557760 | bytes 6695936 | tf_op jit(solution)/shard_map/dot_general | solution.py:81
  134.2 3.6 %collective-permute-start.4 = (bf16[1024,256]{0,1:T(8,128)(2,1)S(1)}, bf16[1024,256]{0,1:T(8,128)(2,1)}, u32[]{:S(2)}, u32[]{:S(2)}) collective-permute-start(bf16[1024,256]{0,1:T(8,128)(2,1)S(1)} %get-tuple-element.24), channel_id=1, source_target_pairs={{0,16},{16,32},{32,48},{48,64},{64,80},{80,96},{96,112},{112,128},... | collective-permute-start | bytes 1572872 | tf_op jit(solution)/shard_map/ppermute | solution.py:27
  139.0 3.1 %collective-permute-start.6 = (bf16[1024,64]{0,1:T(8,128)(2,1)S(1)}, bf16[1024,64]{0,1:T(8,128)(2,1)}, u32[]{:S(2)}, u32[]{:S(2)}) collective-permute-start(bf16[1024,64]{0,1:T(8,128)(2,1)S(1)} %get-tuple-element.14), channel_id=1, source_target_pairs={{0,1},{1,2},{2,3},{3,4},{4,5},{5,6},{6,7},{7,8},{8,9},{9,10},{10,1... | collective-permute-start | bytes 393224 | tf_op jit(solution)/shard_map/ppermute | solution.py:27
  142.0 5.2 %collective-permute-start.7 = (bf16[1024,64]{0,1:T(8,128)(2,1)S(1)}, bf16[1024,64]{0,1:T(8,128)(2,1)}, u32[]{:S(2)}, u32[]{:S(2)}) collective-permute-start(bf16[1024,64]{0,1:T(8,128)(2,1)S(1)} %get-tuple-element.15), channel_id=1, source_target_pairs={{1,0},{2,1},{3,2},{4,3},{5,4},{6,5},{7,6},{8,7},{9,8},{10,9},{11,1... | collective-permute-start | bytes 393224 | tf_op jit(solution)/shard_map/ppermute | solution.py:28
  152.8 2.7 convolution_add_fusion.7
  159.3 4.4 %fusion.86 = (bf16[1024,256]{0,1:T(8,128)(2,1)}, f32[1024,256]{0,1:T(8,128)}) fusion(f32[1024,256]{0,1:T(8,128)} %get-tuple-element.25, f32[1024,256]{0,1:T(8,128)} %copy-done.8, f32[1024,256]{0,1:T(8,128)} %fusion.4, bf16[1024,64]{0,1:T(8,128)(2,1)} %collective-permute-done.7, bf16[1024,256]{0,1:T(8,128)(2,1)S(1)} %get-tuple-element.24, ...), kind=kOutput, calls=%fused_computation.163 | convolution fusion | flops 140247040 | bytes 7735296 | tf_op jit(solution)/shard_map/dot_general | solution.py:81
  165.8 3.5 %collective-permute-start.8 = (bf16[1024,256]{0,1:T(8,128)(2,1)}, bf16[1024,256]{0,1:T(8,128)(2,1)}, u32[]{:S(2)}, u32[]{:S(2)}) collective-permute-start(bf16[1024,256]{0,1:T(8,128)(2,1)} %get-tuple-element.26), channel_id=1, source_target_pairs={{0,16},{16,32},{32,48},{48,64},{64,80},{80,96},{96,112},{112,128},... | collective-permute-start | bytes 1572872 | tf_op jit(solution)/shard_map/ppermute | solution.py:27
  174.8 6.3 %collective-permute-start.11 = (bf16[1024,64]{0,1:T(8,128)(2,1)S(1)}, bf16[1024,64]{0,1:T(8,128)(2,1)}, u32[]{:S(2)}, u32[]{:S(2)}) collective-permute-start(bf16[1024,64]{0,1:T(8,128)(2,1)S(1)} %get-tuple-element.13), channel_id=1, source_target_pairs={{1,0},{2,1},{3,2},{4,3},{5,4},{6,5},{7,6},{8,7},{9,8},{10,9},{11,1... | collective-permute-start | bytes 393224 | tf_op jit(solution)/shard_map/ppermute | solution.py:28
  181.1 2.8 fusion.33
  185.8 2.7 convolution_add_fusion.5
  190.5 4.7 %fusion.87 = (bf16[1024,256]{0,1:T(8,128)(2,1)S(1)}, f32[1024,256]{0,1:T(8,128)}) fusion(f32[1024,256]{0,1:T(8,128)} %get-tuple-element.27, f32[1024,256]{0,1:T(8,128)} %copy-done.8, f32[1024,256]{0,1:T(8,128)} %fusion.3, bf16[1024,64]{0,1:T(8,128)(2,1)} %collective-permute-done.11, bf16[1024,256]{0,1:T(8,128)(2,1)} %get-tuple-element.26, ...), kind=kOutput, calls=%fused_computation.164 | convolution fusion | flops 140247040 | bytes 7735296 | tf_op jit(solution)/shard_map/dot_general | solution.py:81
  197.3 3.7 %collective-permute-start.12 = (bf16[1024,256]{0,1:T(8,128)(2,1)S(1)}, bf16[1024,256]{0,1:T(8,128)(2,1)}, u32[]{:S(2)}, u32[]{:S(2)}) collective-permute-start(bf16[1024,256]{0,1:T(8,128)(2,1)S(1)} %get-tuple-element.28), channel_id=1, source_target_pairs={{0,16},{16,32},{32,48},{48,64},{64,80},{80,96},{96,112},{112,128},... | collective-permute-start | bytes 1572872 | tf_op jit(solution)/shard_map/ppermute | solution.py:27
  204.2 6.3 %collective-permute-start.15 = (bf16[1024,64]{0,1:T(8,128)(2,1)S(1)}, bf16[1024,64]{0,1:T(8,128)(2,1)}, u32[]{:S(2)}, u32[]{:S(2)}) collective-permute-start(bf16[1024,64]{0,1:T(8,128)(2,1)S(1)} %get-tuple-element.11), channel_id=1, source_target_pairs={{1,0},{2,1},{3,2},{4,3},{5,4},{6,5},{7,6},{8,7},{9,8},{10,9},{11,1... | collective-permute-start | bytes 393224 | tf_op jit(solution)/shard_map/ppermute | solution.py:28
  216.0 2.7 convolution_add_fusion.3
  222.6 4.5 %fusion.88 = (bf16[1024,256]{0,1:T(8,128)(2,1)}, f32[1024,256]{0,1:T(8,128)}) fusion(f32[1024,256]{0,1:T(8,128)} %get-tuple-element.29, f32[1024,256]{0,1:T(8,128)} %copy-done.8, f32[1024,256]{0,1:T(8,128)} %fusion.2, bf16[1024,64]{0,1:T(8,128)(2,1)} %collective-permute-done.15, bf16[1024,256]{0,1:T(8,128)(2,1)S(1)} %get-tuple-element.28, ...), kind=kOutput, calls=%fused_computation.165 | convolution fusion | flops 140247040 | bytes 7735296 | tf_op jit(solution)/shard_map/dot_general | solution.py:81
  230.1 4.5 %collective-permute-start.16 = (bf16[1024,256]{0,1:T(8,128)(2,1)}, bf16[1024,256]{0,1:T(8,128)(2,1)}, u32[]{:S(2)}, u32[]{:S(2)}) collective-permute-start(bf16[1024,256]{0,1:T(8,128)(2,1)} %get-tuple-element.30), channel_id=1, source_target_pairs={{0,16},{16,32},{32,48},{48,64},{64,80},{80,96},{96,112},{112,128},... | collective-permute-start | bytes 1572872 | tf_op jit(solution)/shard_map/ppermute | solution.py:27
  236.5 6.4 %collective-permute-start.19 = (bf16[1024,64]{0,1:T(8,128)(2,1)S(1)}, bf16[1024,64]{0,1:T(8,128)(2,1)S(1)}, u32[]{:S(2)}, u32[]{:S(2)}) collective-permute-start(bf16[1024,64]{0,1:T(8,128)(2,1)S(1)} %get-tuple-element.9), channel_id=1, source_target_pairs={{1,0},{2,1},{3,2},{4,3},{5,4},{6,5},{7,6},{8,7},{9,8},{10,9},{11,1... | collective-permute-start | bytes 393224 | tf_op jit(solution)/shard_map/ppermute | solution.py:28
  242.9 2.7 fusion.39
  257.1 32.4 %psum.7 = f32[2,256]{1,0:T(2,128)S(1)} all-reduce(f32[2,256]{1,0:T(2,128)S(1)} %pad_maximum_fusion.10), channel_id=1, replica_groups=mesh['space'=16,'tm'=16] {'space'}, use_global_device_ids=true, to_apply=%region_8.9 | all-reduce | flops 512 | bytes 4096 | tf_op jit(solution)/shard_map/psum | solution.py:138
  (145 shorter events, 79.7 us)
Async XLA Ops:
  0.6 63.5 %copy-start = (bf16[8,8,128,128]{3,2,1,0:T(8,128)(2,1)S(1)}, bf16[8,8,128,128]{3,2,1,0:T(8,128)(2,1)}, u32[]{:S(2)}) copy-start(bf16[8,8,128,128]{3,2,1,0:T(8,128)(2,1)} %param.17) | copy-start | bytes 6291460
  17.0 17.9 %all-to-all-start = ((s32[16,256,1]{1,2,0:T(1,128)}), s32[16,256,1]{1,2,0:T(1,128)S(1)}, u32[]{:S(2)}, u32[]{:S(2)}) async-start(s32[16,256,1]{1,2,0:T(1,128)} %bitcast.15), calls=%async_computation | async-start | bytes 32768 | tf_op jit(solution)/shard_map/all_to_all | solution.py:106
  34.9 61.0 %all-to-all-start.1 = ((bf16[16,256,256]{2,1,0:T(8,128)(2,1)}), bf16[16,256,256]{2,1,0:T(8,128)(2,1)}, u32[]{:S(2)}, u32[]{:S(2)}) async-start(bf16[16,256,256]{2,1,0:T(8,128)(2,1)} %bitcast.111), calls=%async_computation.1 | async-start | bytes 4194304 | tf_op jit(solution)/shard_map/all_to_all | solution.py:105
  40.9 87.0 %copy-start.15 = (f32[256]{0:T(256)}, f32[256]{0:T(256)S(1)}, u32[]{:S(2)}) copy-start(f32[256]{0:T(256)S(1)} %mul.135) | copy-start | bytes 3076
  41.1 86.9 %copy-start.17 = (f32[256]{0:T(256)}, f32[256]{0:T(256)S(1)}, u32[]{:S(2)}) copy-start(f32[256]{0:T(256)S(1)} %broadcast_in_dim_reshape.2) | copy-start | bytes 3076
  41.3 22.8 %copy-start.19 = (s32[8,8]{1,0:T(8,128)S(1)}, s32[8,8]{1,0:T(8,128)}, u32[]{:S(2)}) copy-start(s32[8,8]{1,0:T(8,128)} %param.18) | copy-start | bytes 772
  47.7 41.9 %collective-permute-start.1 = (bf16[1024,256]{0,1:T(8,128)(2,1)}, bf16[1024,256]{0,1:T(8,128)(2,1)}, u32[]{:S(2)}, u32[]{:S(2)}) collective-permute-start(bf16[1024,256]{0,1:T(8,128)(2,1)} %fusion.57), channel_id=1, source_target_pairs={{16,0},{32,16},{48,32},{64,48},{80,64},{96,80},{112,96},{128,112},... | collective-permute-start | bytes 1572872 | tf_op jit(solution)/shard_map/ppermute | solution.py:28
  49.7 41.6 %collective-permute-start = (bf16[1024,256]{0,1:T(8,128)(2,1)}, bf16[1024,256]{0,1:T(8,128)(2,1)}, u32[]{:S(2)}, u32[]{:S(2)}) collective-permute-start(bf16[1024,256]{0,1:T(8,128)(2,1)} %fusion.57), channel_id=1, source_target_pairs={{0,16},{16,32},{32,48},{48,64},{64,80},{80,96},{96,112},{112,128},... | collective-permute-start | bytes 1572872 | tf_op jit(solution)/shard_map/ppermute | solution.py:27
  54.9 73.0 %collective-permute-start.2 = (bf16[1024,64]{0,1:T(8,128)(2,1)}, bf16[1024,64]{0,1:T(8,128)(2,1)}, u32[]{:S(2)}, u32[]{:S(2)}) collective-permute-start(bf16[1024,64]{0,1:T(8,128)(2,1)} %get-tuple-element.16), channel_id=1, source_target_pairs={{0,1},{1,2},{2,3},{3,4},{4,5},{5,6},{6,7},{7,8},{8,9},{9,10},{10,1... | collective-permute-start | bytes 393224 | tf_op jit(solution)/shard_map/ppermute | solution.py:27
  59.8 68.2 %collective-permute-start.3 = (bf16[1024,64]{0,1:T(8,128)(2,1)}, bf16[1024,64]{0,1:T(8,128)(2,1)}, u32[]{:S(2)}, u32[]{:S(2)}) collective-permute-start(bf16[1024,64]{0,1:T(8,128)(2,1)} %get-tuple-element.17), channel_id=1, source_target_pairs={{1,0},{2,1},{3,2},{4,3},{5,4},{6,5},{7,6},{8,7},{9,8},{10,9},{11,1... | collective-permute-start | bytes 393224 | tf_op jit(solution)/shard_map/ppermute | solution.py:28
  68.1 22.7 %copy-start.14 = (s32[1024]{0:T(1024)}, s32[1024]{0:T(1024)S(1)}, u32[]{:S(2)}) copy-start(s32[1024]{0:T(1024)S(1)} %pad_clamp_fusion) | copy-start | bytes 12292
  68.1 24.5 %copy-start.13 = (s32[1024]{0:T(1024)}, s32[1024]{0:T(1024)S(1)}, u32[]{:S(2)}) copy-start(s32[1024]{0:T(1024)S(1)} %pad_clamp_fusion.1) | copy-start | bytes 12292
  128.0 19.3 %copy-start.3 = (bf16[128,8,12,128]{3,1,2,0:T(8,128)(2,1)S(1)}, bf16[128,8,12,128]{3,1,2,0:T(8,128)(2,1)}, u32[]{:S(2)}) copy-start(bf16[128,8,12,128]{3,1,2,0:T(8,128)(2,1)} %copy-done.2) | copy-start | bytes 9437188
  132.2 23.3 %collective-permute-start.5 = (bf16[1024,256]{0,1:T(8,128)(2,1)S(1)}, bf16[1024,256]{0,1:T(8,128)(2,1)}, u32[]{:S(2)}, u32[]{:S(2)}) collective-permute-start(bf16[1024,256]{0,1:T(8,128)(2,1)S(1)} %get-tuple-element.24), channel_id=1, source_target_pairs={{16,0},{32,16},{48,32},{64,48},{80,64},{96,80},{112,96},{128,112},... | collective-permute-start | bytes 1572872 | tf_op jit(solution)/shard_map/ppermute | solution.py:28
  134.2 14.9 %collective-permute-start.4 = (bf16[1024,256]{0,1:T(8,128)(2,1)S(1)}, bf16[1024,256]{0,1:T(8,128)(2,1)}, u32[]{:S(2)}, u32[]{:S(2)}) collective-permute-start(bf16[1024,256]{0,1:T(8,128)(2,1)S(1)} %get-tuple-element.24), channel_id=1, source_target_pairs={{0,16},{16,32},{32,48},{48,64},{64,80},{80,96},{96,112},{112,128},... | collective-permute-start | bytes 1572872 | tf_op jit(solution)/shard_map/ppermute | solution.py:27
  139.0 20.3 %collective-permute-start.6 = (bf16[1024,64]{0,1:T(8,128)(2,1)S(1)}, bf16[1024,64]{0,1:T(8,128)(2,1)}, u32[]{:S(2)}, u32[]{:S(2)}) collective-permute-start(bf16[1024,64]{0,1:T(8,128)(2,1)S(1)} %get-tuple-element.14), channel_id=1, source_target_pairs={{0,1},{1,2},{2,3},{3,4},{4,5},{5,6},{6,7},{7,8},{8,9},{9,10},{10,1... | collective-permute-start | bytes 393224 | tf_op jit(solution)/shard_map/ppermute | solution.py:27
  142.0 17.3 %collective-permute-start.7 = (bf16[1024,64]{0,1:T(8,128)(2,1)S(1)}, bf16[1024,64]{0,1:T(8,128)(2,1)}, u32[]{:S(2)}, u32[]{:S(2)}) collective-permute-start(bf16[1024,64]{0,1:T(8,128)(2,1)S(1)} %get-tuple-element.15), channel_id=1, source_target_pairs={{1,0},{2,1},{3,2},{4,3},{5,4},{6,5},{7,6},{8,7},{9,8},{10,9},{11,1... | collective-permute-start | bytes 393224 | tf_op jit(solution)/shard_map/ppermute | solution.py:28
  159.3 21.7 %copy-start.4 = (bf16[128,8,12,128]{3,1,2,0:T(8,128)(2,1)S(1)}, bf16[128,8,12,128]{3,1,2,0:T(8,128)(2,1)}, u32[]{:S(2)}) copy-start(bf16[128,8,12,128]{3,1,2,0:T(8,128)(2,1)} %copy-done.2) | copy-start | bytes 9437188
  163.8 24.7 %collective-permute-start.9 = (bf16[1024,256]{0,1:T(8,128)(2,1)}, bf16[1024,256]{0,1:T(8,128)(2,1)}, u32[]{:S(2)}, u32[]{:S(2)}) collective-permute-start(bf16[1024,256]{0,1:T(8,128)(2,1)} %get-tuple-element.26), channel_id=1, source_target_pairs={{16,0},{32,16},{48,32},{64,48},{80,64},{96,80},{112,96},{128,112},... | collective-permute-start | bytes 1572872 | tf_op jit(solution)/shard_map/ppermute | solution.py:28
  165.8 18.0 %collective-permute-start.8 = (bf16[1024,256]{0,1:T(8,128)(2,1)}, bf16[1024,256]{0,1:T(8,128)(2,1)}, u32[]{:S(2)}, u32[]{:S(2)}) collective-permute-start(bf16[1024,256]{0,1:T(8,128)(2,1)} %get-tuple-element.26), channel_id=1, source_target_pairs={{0,16},{16,32},{32,48},{48,64},{64,80},{80,96},{96,112},{112,128},... | collective-permute-start | bytes 1572872 | tf_op jit(solution)/shard_map/ppermute | solution.py:27
  172.5 17.9 %collective-permute-start.10 = (bf16[1024,64]{0,1:T(8,128)(2,1)S(1)}, bf16[1024,64]{0,1:T(8,128)(2,1)}, u32[]{:S(2)}, u32[]{:S(2)}) collective-permute-start(bf16[1024,64]{0,1:T(8,128)(2,1)S(1)} %get-tuple-element.12), channel_id=1, source_target_pairs={{0,1},{1,2},{2,3},{3,4},{4,5},{5,6},{6,7},{7,8},{8,9},{9,10},{10,1... | collective-permute-start | bytes 393224 | tf_op jit(solution)/shard_map/ppermute | solution.py:27
  174.8 15.7 %collective-permute-start.11 = (bf16[1024,64]{0,1:T(8,128)(2,1)S(1)}, bf16[1024,64]{0,1:T(8,128)(2,1)}, u32[]{:S(2)}, u32[]{:S(2)}) collective-permute-start(bf16[1024,64]{0,1:T(8,128)(2,1)S(1)} %get-tuple-element.13), channel_id=1, source_target_pairs={{1,0},{2,1},{3,2},{4,3},{5,4},{6,5},{7,6},{8,7},{9,8},{10,9},{11,1... | collective-permute-start | bytes 393224 | tf_op jit(solution)/shard_map/ppermute | solution.py:28
  190.5 20.0 %copy-start.5 = (bf16[128,8,12,128]{3,1,2,0:T(8,128)(2,1)S(1)}, bf16[128,8,12,128]{3,1,2,0:T(8,128)(2,1)}, u32[]{:S(2)}) copy-start(bf16[128,8,12,128]{3,1,2,0:T(8,128)(2,1)} %copy-done.2) | copy-start | bytes 9437188
  195.2 23.6 %collective-permute-start.13 = (bf16[1024,256]{0,1:T(8,128)(2,1)S(1)}, bf16[1024,256]{0,1:T(8,128)(2,1)}, u32[]{:S(2)}, u32[]{:S(2)}) collective-permute-start(bf16[1024,256]{0,1:T(8,128)(2,1)S(1)} %get-tuple-element.28), channel_id=1, source_target_pairs={{16,0},{32,16},{48,32},{64,48},{80,64},{96,80},{112,96},{128,112},... | collective-permute-start | bytes 1572872 | tf_op jit(solution)/shard_map/ppermute | solution.py:28
  197.3 14.9 %collective-permute-start.12 = (bf16[1024,256]{0,1:T(8,128)(2,1)S(1)}, bf16[1024,256]{0,1:T(8,128)(2,1)}, u32[]{:S(2)}, u32[]{:S(2)}) collective-permute-start(bf16[1024,256]{0,1:T(8,128)(2,1)S(1)} %get-tuple-element.28), channel_id=1, source_target_pairs={{0,16},{16,32},{32,48},{48,64},{64,80},{80,96},{96,112},{112,128},... | collective-permute-start | bytes 1572872 | tf_op jit(solution)/shard_map/ppermute | solution.py:27
  202.2 20.3 %collective-permute-start.14 = (bf16[1024,64]{0,1:T(8,128)(2,1)S(1)}, bf16[1024,64]{0,1:T(8,128)(2,1)}, u32[]{:S(2)}, u32[]{:S(2)}) collective-permute-start(bf16[1024,64]{0,1:T(8,128)(2,1)S(1)} %get-tuple-element.10), channel_id=1, source_target_pairs={{0,1},{1,2},{2,3},{3,4},{4,5},{5,6},{6,7},{7,8},{8,9},{9,10},{10,1... | collective-permute-start | bytes 393224 | tf_op jit(solution)/shard_map/ppermute | solution.py:27
  204.2 18.4 %collective-permute-start.15 = (bf16[1024,64]{0,1:T(8,128)(2,1)S(1)}, bf16[1024,64]{0,1:T(8,128)(2,1)}, u32[]{:S(2)}, u32[]{:S(2)}) collective-permute-start(bf16[1024,64]{0,1:T(8,128)(2,1)S(1)} %get-tuple-element.11), channel_id=1, source_target_pairs={{1,0},{2,1},{3,2},{4,3},{5,4},{6,5},{7,6},{8,7},{9,8},{10,9},{11,1... | collective-permute-start | bytes 393224 | tf_op jit(solution)/shard_map/ppermute | solution.py:28
  222.6 20.3 %copy-start.6 = (bf16[128,8,12,128]{3,1,2,0:T(8,128)(2,1)S(1)}, bf16[128,8,12,128]{3,1,2,0:T(8,128)(2,1)}, u32[]{:S(2)}) copy-start(bf16[128,8,12,128]{3,1,2,0:T(8,128)(2,1)} %copy-done.2) | copy-start | bytes 9437188
  228.1 21.9 %collective-permute-start.17 = (bf16[1024,256]{0,1:T(8,128)(2,1)}, bf16[1024,256]{0,1:T(8,128)(2,1)}, u32[]{:S(2)}, u32[]{:S(2)}) collective-permute-start(bf16[1024,256]{0,1:T(8,128)(2,1)} %get-tuple-element.30), channel_id=1, source_target_pairs={{16,0},{32,16},{48,32},{64,48},{80,64},{96,80},{112,96},{128,112},... | collective-permute-start | bytes 1572872 | tf_op jit(solution)/shard_map/ppermute | solution.py:28
  230.1 21.8 %collective-permute-start.16 = (bf16[1024,256]{0,1:T(8,128)(2,1)}, bf16[1024,256]{0,1:T(8,128)(2,1)}, u32[]{:S(2)}, u32[]{:S(2)}) collective-permute-start(bf16[1024,256]{0,1:T(8,128)(2,1)} %get-tuple-element.30), channel_id=1, source_target_pairs={{0,16},{16,32},{32,48},{48,64},{64,80},{80,96},{96,112},{112,128},... | collective-permute-start | bytes 1572872 | tf_op jit(solution)/shard_map/ppermute | solution.py:27
  234.6 13.6 %collective-permute-start.18 = (bf16[1024,64]{0,1:T(8,128)(2,1)S(1)}, bf16[1024,64]{0,1:T(8,128)(2,1)S(1)}, u32[]{:S(2)}, u32[]{:S(2)}) collective-permute-start(bf16[1024,64]{0,1:T(8,128)(2,1)S(1)} %get-tuple-element.8), channel_id=1, source_target_pairs={{0,1},{1,2},{2,3},{3,4},{4,5},{5,6},{6,7},{7,8},{8,9},{9,10},{10,1... | collective-permute-start | bytes 393224 | tf_op jit(solution)/shard_map/ppermute | solution.py:27
  236.5 11.7 %collective-permute-start.19 = (bf16[1024,64]{0,1:T(8,128)(2,1)S(1)}, bf16[1024,64]{0,1:T(8,128)(2,1)S(1)}, u32[]{:S(2)}, u32[]{:S(2)}) collective-permute-start(bf16[1024,64]{0,1:T(8,128)(2,1)S(1)} %get-tuple-element.9), channel_id=1, source_target_pairs={{1,0},{2,1},{3,2},{4,3},{5,4},{6,5},{7,6},{8,7},{9,8},{10,9},{11,1... | collective-permute-start | bytes 393224 | tf_op jit(solution)/shard_map/ppermute | solution.py:28
  (13 other events, 117.6 us)
where the time goes:
time: 294 us; the launch traced here: 290 us
  starting transfers between devices  83.8 us (29%)
  local copies, waits for them, and re-layouts  79.6 us (27%)
  other arithmetic  46.8 us (16%)
  matrix products  46 us (16%)
  blocking collectives  32.4 us (11%)
    ppermute x10, starting transfers between devices, with_halo(): after = lax.ppermute(initial, axis, down)  38.5 us
    ppermute x10, starting transfers between devices, with_halo(): before = lax.ppermute(last, axis, up)  32.9 us
    psum x1, blocking collectives, shards(): totals = lax.psum(partial_sums, 'space')  32.4 us
    scatter-add x1, other arithmetic, shards(): jax.ops.segment_sum(obs_weight, cell_ids, num_segments=NODES_DEV * T_DEV)  27 us
    dot_general x5, matrix products, spatial(): jnp.dot(upper_part, upper, preferred_element_type=jnp.float32)  19.4 us
    gather x1, local copies, waits for them, and re-layouts, shards(): coef_rows = svc_coef[cell_ids // T_DEV]  17 us
    dot_general x5, matrix products, spatial(): jnp.dot(lower_part, lower, preferred_element_type=jnp.float32)  12.7 us
    dot_general x5, matrix products, spatial(): total = jnp.dot(own_part, field, preferred_element_type=jnp.float32)  11.8 us
  transfers between devices with their start and end apart: 22, of which 0 were waited for; matrix products, arithmetic and copies ran while one was open for 45% of the time, Pallas kernels for 0%

commit v1 on v0

v1 whole, which is shorter than its diff:
```python
import functools

import jax
import jax.numpy as jnp
from jax import lax
from jax.experimental import pallas as pl
from jax.experimental.pallas import tpu as pltpu
from jax.sharding import PartitionSpec as P

NB_DEV = 8
BLOCK = 128
HALO_B = 2
T_DEV = 4
PROBES = 64
NCOV = 256
OBS_DEV = 2048
ITERS = 4
NODES_DEV = 1024
COLS = T_DEV * PROBES
WIDTH = (NB_DEV + 2 * HALO_B) * BLOCK
HALO_ROWS = HALO_B * BLOCK
PACKED = NODES_DEV // 2
ROWS = NCOV + 16
EXCHANGES = ITERS + 1
CHUNK = 256

RELAX = 0.6
MESH = pl.DeviceIdType.MESH
F32 = jnp.float32
BF16 = jnp.bfloat16
NT_DIMS = (((1,), (1,)), ((), ()))


def dot(a, b):
    return jnp.dot(a, b, preferred_element_type=F32)


def iota(shape, dim):
    return lax.broadcasted_iota(jnp.int32, shape, dim)


def mark(condition):
    return jnp.where(condition, 1.0, 0.0).astype(BF16)


def split3(values):
    first = jnp.clip(values, -3.38e38, 3.38e38).astype(BF16)
    rest = values - first.astype(F32)
    second = rest.astype(BF16)
    third = (rest - second.astype(F32)).astype(BF16)
    return first, second, third


def kernel(
    peers,
    slabs,
    cap,
    probe_hbm,
    kappa_ref,
    theta_space_ref,
    theta_time_ref,
    diag_hbm,
    off_hbm,
    cols_ref,
    needs_ref,
    cov_hbm,
    owner_ref,
    cell_ref,
    coef_hbm,
    sol_ref,
    grads_ref,
    probe,
    diag,
    off,
    cov,
    coef,
    slots,
    covt,
    onehot,
    send_obs,
    recv_obs,
    masks,
    counted,
    comb,
    field,
    time_low,
    time_high,
    send_up,
    send_down,
    send_left,
    send_right,
    product,
    local_diag,
    step,
    needs_out,
    needs_in,
    picks,
    grads_out,
    grads_in,
    load_sem,
    obs_send_sem,
    obs_recv_sem,
    needs_send_sem,
    needs_recv_sem,
    halo_send_sem,
    halo_recv_sem,
    grads_send_sem,
    grads_recv_sem,
):
    me = lax.axis_index("space")
    slab = lax.axis_index("tm")
    left = lax.rem(slab + slabs - 1, slabs)
    right = lax.rem(slab + 1, slabs)
    down = lax.rem(me + peers - 1, peers)
    up = lax.rem(me + 1, peers)
    has_down, has_up = me > 0, me < peers - 1
    has_left, has_right = slab > 0, slab < slabs - 1

    loads = [
        pltpu.make_async_copy(src, dst, load_sem.at[i])
        for i, (src, dst) in enumerate(
            ((cov_hbm, cov), (probe_hbm, probe), (diag_hbm, diag), (off_hbm, off), (coef_hbm, coef))
        )
    ]
    for load in loads:
        load.start()

    barrier = pltpu.get_barrier_semaphore()

    def greet(k, carry):
        pl.semaphore_signal(
            barrier, inc=1, device_id=(lax.rem(me + k, peers), slab), device_id_type=MESH
        )
        return carry

    lax.fori_loop(1, peers, greet, 0)
    for other in (left, right):
        pl.semaphore_signal(barrier, inc=1, device_id=(me, other), device_id_type=MESH)

    owner_cols = jnp.transpose(owner_ref[...].astype(F32))
    lanes = iota((BLOCK, BLOCK), 1)
    below = mark(iota((BLOCK, BLOCK), 1) < iota((BLOCK, BLOCK), 0))
    seen = jnp.zeros((1, BLOCK), F32)
    for c in range(OBS_DEV // BLOCK):
        owner_col = owner_cols[:, c : c + 1].astype(jnp.int32)
        hit = owner_col == lanes
        hits = mark(hit)
        before = dot(below, hits) + seen
        rank = jnp.sum(jnp.where(hit, before, 0.0), axis=1, keepdims=True)
        seen = seen + jnp.sum(hits.astype(F32), axis=0, keepdims=True)
        slot = owner_col * cap + rank.astype(jnp.int32)
        slots[c * BLOCK : (c + 1) * BLOCK, :] = jnp.broadcast_to(slot, (BLOCK, BLOCK))

    loads[0].wait()
    sub = iota((16, BLOCK), 0)
    for c in range(OBS_DEV // BLOCK):
        part = slice(c * BLOCK, (c + 1) * BLOCK)
        covt[:NCOV, part] = jnp.transpose(cov[part, :])
        cell = jnp.broadcast_to(cell_ref[c : c + 1, :], (16, BLOCK))
        extra = jnp.where(
            sub == 0, cell // 64, jnp.where(sub == 1, cell % 64, jnp.where(sub == 2, 1, 0))
        )
        covt[NCOV:, part] = extra.astype(F32).astype(BF16)

    def compact(target):
        for c in range(OBS_DEV // BLOCK):
            part = slice(c * BLOCK, (c + 1) * BLOCK)
            place = slots[part, :] - target * cap
            for h in range(0, cap, BLOCK):
                onehot[part, h : h + BLOCK] = mark(place == lanes + h)
        return dot(covt[...], onehot[...]).astype(BF16)

    pl.semaphore_wait(barrier, peers + 1)

    sub8 = iota((8, COLS), 0)
    listed = jnp.zeros((8, COLS), jnp.int32)
    for i in range(2 * HALO_B):
        listed = jnp.where(sub8 == i, needs_ref[i], listed)
    needs_out[...] = listed

    def needs_copy(side, target):
        return pltpu.make_async_remote_copy(
            src_ref=needs_out,
            dst_ref=needs_in.at[side],
            send_sem=needs_send_sem.at[side],
            recv_sem=needs_recv_sem.at[side],
            device_id=(target, slab),
            device_id_type=MESH,
        )

    needs_copies = (needs_copy(0, up), needs_copy(1, down))
    for copy in needs_copies:
        copy.start()

    def obs_copy(k, target):
        return pltpu.make_async_remote_copy(
            src_ref=send_obs.at[k],
            dst_ref=recv_obs.at[k],
            send_sem=obs_send_sem.at[k],
            recv_sem=obs_recv_sem.at[k],
            device_id=(target, slab),
            device_id_type=MESH,
        )

    def send(k, carry):
        target = lax.rem(me + k, peers)
        send_obs[k] = compact(target)
        obs_copy(k, target).start()
        return carry

    lax.fori_loop(1, peers, send, 0)
    recv_obs[0] = compact(me)

    col_time = iota((1, COLS), 1) // PROBES
    scale_space = jnp.zeros((1, COLS), F32)
    scale_time = jnp.zeros((1, COLS), F32)
    for t in range(T_DEV):
        scale_space = jnp.where(col_time == t, theta_space_ref[t], scale_space)
        scale_time = jnp.where(col_time == t, theta_time_ref[t], scale_time)
    kappa_cols = jnp.transpose(kappa_ref[...])
    eye = iota((BLOCK, BLOCK), 0) == iota((BLOCK, BLOCK), 1)
    loads[1].wait()
    loads[2].wait()
    for b in range(NB_DEV):
        part = slice(b * BLOCK, (b + 1) * BLOCK)
        sdiag = jnp.sum(jnp.where(eye, diag[b].astype(F32), 0.0), axis=1, keepdims=True)
        kappa_col = kappa_cols[:, b : b + 1]
        base = scale_space * sdiag + 2.0 * scale_time + kappa_col
        step[part, :] = base
        local_diag[part, :] = jnp.broadcast_to(kappa_col, (BLOCK, COLS))
        start = RELAX * probe[part, :].astype(F32) / base
        sol_ref[part, :] = start
        field[0, part, :] = start.astype(BF16)

    for e in range(EXCHANGES):

        @pl.when(jnp.logical_not(has_down))
        def _():
            field[e, NODES_DEV : NODES_DEV + HALO_ROWS, :] = jnp.zeros((HALO_ROWS, COLS), BF16)

        @pl.when(jnp.logical_not(has_up))
        def _():
            field[e, NODES_DEV + HALO_ROWS :, :] = jnp.zeros((HALO_ROWS, COLS), BF16)

        @pl.when(jnp.logical_not(has_left))
        def _():
            time_low[e] = jnp.zeros((PACKED, BLOCK), BF16)

        @pl.when(jnp.logical_not(has_right))
        def _():
            time_high[e] = jnp.zeros((PACKED, BLOCK), BF16)

    for copy in needs_copies:
        copy.wait()
    for i in range(HALO_B):
        for b in range(NB_DEV):
            for side, row in ((1, i), (0, HALO_B + i)):
                picks[side, i, b] = mark(needs_in[side, row : row + 1, :] == b)

    row128 = iota((BLOCK, BLOCK), 0)
    shift_low = mark(row128 == lanes + PROBES)
    keep_high = mark((row128 == lanes) & (lanes >= PROBES))
    keep_low = mark((row128 == lanes) & (lanes < PROBES))
    shift_high = mark(row128 + PROBES == lanes)

    def halo_copy(e, which, src, dst, target):
        return pltpu.make_async_remote_copy(
            src_ref=src,
            dst_ref=dst,
            send_sem=halo_send_sem.at[e, which],
            recv_sem=halo_recv_sem.at[e, which],
            device_id=target,
            device_id_type=MESH,
        )

    def halo_copies(e):
        low = field.at[e, pl.ds(NODES_DEV, HALO_ROWS)]
        high = field.at[e, pl.ds(NODES_DEV + HALO_ROWS, HALO_ROWS)]
        return (
            (has_right, has_left, halo_copy(e, 0, send_right.at[e], time_low.at[e], (me, right))),
            (has_left, has_right, halo_copy(e, 1, send_left.at[e], time_high.at[e], (me, left))),
            (has_up, has_down, halo_copy(e, 2, send_up.at[e], low, (up, slab))),
            (has_down, has_up, halo_copy(e, 3, send_down.at[e], high, (down, slab))),
        )

    def start_halo(e):
        send_right[e] = (
            dot(field[e, :PACKED, BLOCK:], shift_low) + dot(field[e, PACKED:NODES_DEV, BLOCK:], keep_high)
        ).astype(BF16)
        send_left[e] = (
            dot(field[e, :PACKED, :BLOCK], keep_low) + dot(field[e, PACKED:NODES_DEV, :BLOCK], shift_high)
        ).astype(BF16)
        for i in range(HALO_B):
            part = slice(i * BLOCK, (i + 1) * BLOCK)
            for side, staged in ((1, send_up), (0, send_down)):
                chosen = picks[side, i, 0] * field[e, :BLOCK, :]
                for b in range(1, NB_DEV):
                    chosen = chosen + picks[side, i, b] * field[e, b * BLOCK : (b + 1) * BLOCK, :]
                staged[e, part, :] = chosen
        for sends, _, copy in halo_copies(e):
            pl.when(sends)(copy.start)

    def wait_halo(e):
        for _, receives, copy in halo_copies(e):
            pl.when(receives)(copy.wait_recv)

    start_halo(0)

    loads[3].wait()

    def combine(i, carry):
        b = i // NB_DEV
        rows = pl.ds(pl.multiple_of((i % NB_DEV) * 16, 16), 16)
        parts = [off[b, k, rows, :].astype(F32) for k in range(NB_DEV)]
        own = diag[b, rows, :].astype(F32)
        columns = [cols_ref[b, k] for k in range(NB_DEV)]
        place = pl.ds(pl.multiple_of(i * 16, 16), 16)
        for m in range(WIDTH // BLOCK):
            total = jnp.zeros((16, BLOCK), F32)
            for k in range(NB_DEV):
                total = total + jnp.where(columns[k] == m, 1.0, 0.0) * parts[k]
            if m < NB_DEV:
                total = total + jnp.where(b == m, 1.0, 0.0) * own
            comb[place, m * BLOCK : (m + 1) * BLOCK] = total.astype(BF16)
        return carry

    lax.fori_loop(0, NODES_DEV // 16, combine, 0)

    row_t, lane_t = iota((COLS, COLS), 0), iota((COLS, COLS), 1)
    inner = jnp.where(
        row_t == lane_t, 2.0, jnp.where(jnp.abs(row_t - lane_t) == PROBES, -1.0, 0.0)
    ).astype(BF16)
    row_h, lane_h = iota((BLOCK, COLS), 0), iota((BLOCK, COLS), 1)
    low_edge, high_edge = [], []
    for half in range(2):
        chosen = (row_h // PROBES) == half
        shift = half * PROBES
        low_edge.append(jnp.where(chosen & (lane_h == row_h - shift), -1.0, 0.0).astype(BF16))
        high_edge.append(
            jnp.where(chosen & (lane_h == row_h - shift + COLS - PROBES), -1.0, 0.0).astype(BF16)
        )

    def own_product(e):
        product[...] = dot(comb[:, :NODES_DEV], field[e, :NODES_DEV, :])

    def both(e, c):
        part = slice(c * CHUNK, (c + 1) * CHUNK)
        half, rest = divmod(c * CHUNK, PACKED)
        packed = slice(rest, rest + CHUNK)
        space = product[part, :] + dot(comb[part, NODES_DEV:], field[e, NODES_DEV:, :])
        time = (
            dot(field[e, part, :], inner)
            + dot(time_low[e, packed, :], low_edge[half])
            + dot(time_high[e, packed, :], high_edge[half])
        )
        return part, space, time

    own_product(0)

    loads[4].wait()
    counted[...] = jnp.zeros((NODES_DEV, BLOCK), F32)
    row_w = iota((BLOCK, cap), 0)

    def weigh(k):
        digits = recv_obs[k, NCOV:, :].astype(F32)
        live = digits[2:3, :] > 0.5
        cell = (digits[0:1, :] * 64.0 + digits[1:2, :]).astype(jnp.int32)
        node = jnp.where(live, cell // T_DEV, -1)
        time = cell % T_DEV
        rows = recv_obs[k, :NCOV, :]
        eta = jnp.zeros((1, cap), F32)
        for c in range(NODES_DEV // CHUNK):
            part = slice(c * CHUNK, (c + 1) * CHUNK)
            scores = dot(coef[part, :], rows)
            found = iota((CHUNK, cap), 0) + c * CHUNK == node
            eta = eta + jnp.sum(jnp.where(found, scores, 0.0), axis=0, keepdims=True)
            masks[part, :] = mark(found)
        weight = jnp.where(live, jnp.exp(eta), 0.0)
        pieces = [piece.astype(F32) for piece in split3(weight)]
        spread = jnp.zeros((BLOCK, cap), F32)
        for i, piece in enumerate(pieces):
            spread = jnp.where(row_w == time + i * T_DEV, piece, spread)
        counted[...] += lax.dot_general(
            masks[...], spread.astype(BF16), NT_DIMS, preferred_element_type=F32
        )

    weigh(0)

    def receive(k, carry):
        obs_copy(k, lax.rem(me + k, peers)).wait_recv()
        weigh(k)
        return carry

    lax.fori_loop(1, peers, receive, 0)

    spread_row, spread_col = iota((BLOCK, COLS), 0), iota((BLOCK, COLS), 1) // PROBES
    repeat = mark((spread_row < 3 * T_DEV) & (spread_row % T_DEV == spread_col))
    wait_halo(0)
    for c in range(NODES_DEV // CHUNK):
        part, space, time = both(0, c)
        pieces = split3(counted[part, :])
        obs_diag = dot(pieces[0], repeat) + dot(pieces[1], repeat) + dot(pieces[2], repeat)
        mine = local_diag[part, :] + obs_diag
        local_diag[part, :] = mine
        rate = RELAX / (step[part, :] + obs_diag)
        step[part, :] = rate
        applied = scale_space * space + scale_time * time + mine * field[0, part, :].astype(F32)
        solved = sol_ref[part, :] + rate * (probe[part, :].astype(F32) - applied)
        sol_ref[part, :] = solved
        field[1, part, :] = solved.astype(BF16)

    for e in range(1, ITERS):
        start_halo(e)
        own_product(e)
        wait_halo(e)
        for c in range(NODES_DEV // CHUNK):
            part, space, time = both(e, c)
            applied = (
                scale_space * space
                + scale_time * time
                + local_diag[part, :] * field[e, part, :].astype(F32)
            )
            solved = sol_ref[part, :] + step[part, :] * (probe[part, :].astype(F32) - applied)
            sol_ref[part, :] = solved
            field[e + 1, part, :] = solved.astype(BF16)

    start_halo(ITERS)
    own_product(ITERS)
    wait_halo(ITERS)
    sums = [jnp.zeros((1, COLS), F32), jnp.zeros((1, COLS), F32)]
    for c in range(NODES_DEV // CHUNK):
        part, space, time = both(ITERS, c)
        values = probe[part, :].astype(F32)
        sums[0] = sums[0] + jnp.sum(values * space, axis=0, keepdims=True)
        sums[1] = sums[1] + jnp.sum(values * time, axis=0, keepdims=True)
    grads_out[...] = jnp.where(sub8 == 0, sums[0], jnp.where(sub8 == 1, sums[1], 0.0))
    grads_in[me] = grads_out[...]

    def grads_copy(k):
        target = lax.rem(me + k, peers)
        return pltpu.make_async_remote_copy(
            src_ref=grads_out,
            dst_ref=grads_in.at[me],
            send_sem=grads_send_sem.at[k],
            recv_sem=grads_recv_sem.at[k],
            device_id=(target, slab),
            device_id_type=MESH,
        )

    def grads_send(k, carry):
        grads_copy(k).start()
        return carry

    lax.fori_loop(1, peers, grads_send, 0)

    def finish(k, carry):
        grads_copy(k).wait()
        obs_copy(k, lax.rem(me + k, peers)).wait_send()
        return carry

    lax.fori_loop(1, peers, finish, 0)
    for e in range(EXCHANGES):
        for sends, _, copy in halo_copies(e):
            pl.when(sends)(copy.wait_send)
    total = grads_in[0]
    for s in range(1, peers):
        total = total + grads_in[s]
    grads_ref[...] = total[0:2, :] / (NODES_DEV * peers)


def shards(
    probe_field,
    kappa,
    theta_space,
    theta_time,
    diag_blocks,
    off_blocks,
    block_cols,
    halo_needs,
    covariates,
    obs_owner,
    obs_cell,
    svc_coef,
):
    peers = lax.axis_size("space")
    slabs = lax.axis_size("tm")
    cap = 2 * OBS_DEV // peers
    vmem = pl.BlockSpec(memory_space=pltpu.VMEM)
    smem = pl.BlockSpec(memory_space=pltpu.SMEM)
    anywhere = pl.BlockSpec(memory_space=pl.ANY)
    dma = pltpu.SemaphoreType.DMA
    return pl.pallas_call(
        functools.partial(kernel, peers, slabs, cap),
        out_shape=(
            jax.ShapeDtypeStruct((NODES_DEV, COLS), F32),
            jax.ShapeDtypeStruct((2, COLS), F32),
        ),
        in_specs=[
            anywhere,
            vmem,
            smem,
            smem,
            anywhere,
            anywhere,
            smem,
            smem,
            anywhere,
            vmem,
            vmem,
            anywhere,
        ],
        out_specs=(vmem, vmem),
        scratch_shapes=[
            pltpu.VMEM((NODES_DEV, COLS), BF16),
            pltpu.VMEM((NB_DEV, BLOCK, BLOCK), BF16),
            pltpu.VMEM((NB_DEV, NB_DEV, BLOCK, BLOCK), BF16),
            pltpu.VMEM((OBS_DEV, NCOV), BF16),
            pltpu.VMEM((NODES_DEV, NCOV), BF16),
            pltpu.VMEM((OBS_DEV, BLOCK), jnp.int32),
            pltpu.VMEM((ROWS, OBS_DEV), BF16),
            pltpu.VMEM((OBS_DEV, cap), BF16),
            pltpu.VMEM((peers, ROWS, cap), BF16),
            pltpu.VMEM((peers, ROWS, cap), BF16),
            pltpu.VMEM((NODES_DEV, cap), BF16),
            pltpu.VMEM((NODES_DEV, BLOCK), F32),
            pltpu.VMEM((NODES_DEV, WIDTH), BF16),
            pltpu.VMEM((EXCHANGES, WIDTH, COLS), BF16),
            pltpu.VMEM((EXCHANGES, PACKED, BLOCK), BF16),
            pltpu.VMEM((EXCHANGES, PACKED, BLOCK), BF16),
            pltpu.VMEM((EXCHANGES, HALO_ROWS, COLS), BF16),
            pltpu.VMEM((EXCHANGES, HALO_ROWS, COLS), BF16),
            pltpu.VMEM((EXCHANGES, PACKED, BLOCK), BF16),
            pltpu.VMEM((EXCHANGES, PACKED, BLOCK), BF16),
            pltpu.VMEM((NODES_DEV, COLS), F32),
            pltpu.VMEM((NODES_DEV, COLS), F32),
            pltpu.VMEM((NODES_DEV, COLS), F32),
            pltpu.VMEM((8, COLS), jnp.int32),
            pltpu.VMEM((2, 8, COLS), jnp.int32),
            pltpu.VMEM((2, HALO_B, NB_DEV, 1, COLS), BF16),
            pltpu.VMEM((8, COLS), F32),
            pltpu.VMEM((peers, 8, COLS), F32),
            dma((5,)),
            dma((peers,)),
            dma((peers,)),
            dma((2,)),
            dma((2,)),
            dma((EXCHANGES, 4)),
            dma((EXCHANGES, 4)),
            dma((peers,)),
            dma((peers,)),
        ],
        compiler_params=pltpu.CompilerParams(
            collective_id=0,
            has_side_effects=True,
            vmem_limit_bytes=48 * 1024 * 1024,
        ),
    )(
        probe_field,
        kappa.reshape(NB_DEV, BLOCK),
        theta_space,
        theta_time,
        diag_blocks,
        off_blocks,
        block_cols,
        halo_needs,
        covariates,
        obs_owner.reshape(OBS_DEV // BLOCK, BLOCK),
        obs_cell.reshape(OBS_DEV // BLOCK, BLOCK),
        svc_coef,
    )


def solution(mesh):
    return jax.shard_map(
        shards,
        mesh=mesh,
        in_specs=(
            P("space", "tm"),
            P("space"),
            P("tm"),
            P("tm"),
            P("space", None, None),
            P("space", None, None, None),
            P("space", None),
            P("space"),
            P(("space", "tm"), None),
            P(("space", "tm"), None),
            P(("space", "tm")),
            P("space", None),
        ),
        out_specs=(P("space", "tm"), P(None, "tm")),
        check_vma=False,
    )
```

time: 294 us -> 110 us (0.37); the launches traced: 290 us -> 110 us
  Pallas kernels: 0 us -> 96.9 us
  starting transfers between devices: 83.8 us -> 0 us
  local copies, waits for them, and re-layouts: 79.6 us -> 12.1 us
  other arithmetic: 46.8 us -> 0 us
  matrix products: 46 us -> 0 us
  blocking collectives: 32.4 us -> 0 us
    pallas_call x0 -> x1, Pallas kernels: none -> 96.9 us  [shards(): pl.pallas_call(functools.partial(kernel, peers, slabs, cap), out_shape=(j...]
    ppermute x20 -> x0, starting transfers between devices: 71.4 us -> none  [the longest x10 38.5 us: with_halo(): after = lax.ppermute(initial, axis, down)]
    dot_general x16 -> x0, matrix products: 46 us -> none  [the longest x5 19.4 us: spatial(): jnp.dot(upper_part, upper, preferred_element_type=jnp.float32)]
    psum x1 -> x0, blocking collectives: 32.4 us -> none  [shards(): totals = lax.psum(partial_sums, 'space')]
    gather x12 -> x0, local copies, waits for them, and re-layouts: 29.6 us -> none  [the longest x1 17 us: shards(): coef_rows = svc_coef[cell_ids // T_DEV]]
    scatter-add x1 -> x0, other arithmetic: 27 us -> none  [shards(): jax.ops.segment_sum(obs_weight, cell_ids, num_segments=NODES_DEV * T_DEV)]
    scatter x2 -> x0, local copies, waits for them, and re-layouts: 20.1 us -> none  [the longest x1 11.3 us: shards(): jnp.zeros((space_count * capacity, NCOV), jnp.bfloat16).at[slot]]
    reshape x12 -> x0, local copies, waits for them, and re-layouts: 16.4 us -> none  [the longest x5 7.82 us: spatial(): upper = arrived[2 * NODES_DEV:].reshape(NB_DEV, BLOCK, columns)[halo_need...]
  transfers between devices with their start and end apart: 22 -> 0, of which waited for: 0 -> 0; matrix products, arithmetic and copies ran while one was open for 45% -> 0% of each run, Pallas kernels for 0% -> 0%
where the time goes in v1:
time: 110 us
  Pallas kernels  96.9 us (88%)
  local copies, waits for them, and re-layouts  12.1 us (11%)
    pallas_call x1, Pallas kernels, shards(): pl.pallas_call(functools.partial(kernel, peers, slabs, cap), out_shape=(j...  96.9 us
    unnamed x26, local copies, waits for them, and re-layouts  12.1 us

profile of v1, /device:TPU:5, one launch (start us, length us, event | category | flops | bytes accessed | tf_op | source)
XLA Modules:
  0.0 109.7 jit_solution(2849188800050365083)
XLA Ops:
  0.6 0.0 copy-start
  0.6 1.6 %copy-done = bf16[8,8,128,128]{3,2,1,0:T(8,128)(2,1)S(1)} copy-done((bf16[8,8,128,128]{3,2,1,0:T(8,128)(2,1)S(1)}, bf16[8,8,128,128]{3,2,1,0:T(8,128)(2,1)}, u32[]{:S(2)}) %copy-start) | copy-done | bytes 2097176
  2.2 0.0 copy-start.1
  2.2 1.2 %copy-done.1 = bf16[2048,256]{1,0:T(8,128)(2,1)S(1)} copy-done((bf16[2048,256]{1,0:T(8,128)(2,1)S(1)}, bf16[2048,256]{1,0:T(8,128)(2,1)}, u32[]{:S(2)}) %copy-start.1) | copy-done | bytes 1048600
  3.5 0.0 copy-start.2
  3.5 1.0 copy-done.2
  4.5 0.0 copy-start.3
  4.5 1.0 copy-done.3
  5.5 0.0 copy-start.4
  5.5 0.9 copy-done.4
  6.5 0.0 copy-start.5
  6.5 0.7 copy-done.5
  7.2 0.0 copy-start.6
  7.2 0.7 copy-done.6
  7.9 0.0 copy-start.7
  7.9 0.7 copy-done.7
  8.6 0.0 copy-start.8
  8.6 0.7 copy-done.8
  9.3 0.0 copy-start.9
  9.3 0.7 copy-done.9
  9.9 0.0 copy-start.10
  9.9 0.7 copy-done.10
  10.6 0.0 copy-start.11
  10.6 0.7 copy-done.11
  11.2 96.9 %shard_map.131 = (f32[1024,256]{1,0:T(8,128)S(1)}, f32[2,256]{1,0:T(2,128)S(1)}) custom-call(bf16[1024,256]{1,0:T(8,128)(2,1)S(1)} %copy-done.2, f32[8,128]{1,0:T(8,128)S(1)} %bitcast.5, f32[4]{0:T(128)S(1)} %copy-done.9, f32[4]{0:T(128)S(1)} %copy-done.10, bf16[8,128,128]{2,1,0:T(8,128)(2,1)S(1)} %copy-done.4, bf16[8,8,128,128]{3,2,1,0:T(8,128)(2,1)S(1)} %copy-done, ...), custom_call_target="tpu_custom_call" | custom-call | tf_op jit(solution)/shard_map/pallas_call | solution.py:492
  108.1 1.0 copy.16
  109.1 0.6 copy.17
Async XLA Ops:
  0.6 1.6 %copy-start = (bf16[8,8,128,128]{3,2,1,0:T(8,128)(2,1)S(1)}, bf16[8,8,128,128]{3,2,1,0:T(8,128)(2,1)}, u32[]{:S(2)}) copy-start(bf16[8,8,128,128]{3,2,1,0:T(8,128)(2,1)} %off_hbm.1) | copy-start | bytes 6291460
  2.2 1.2 %copy-start.1 = (bf16[2048,256]{1,0:T(8,128)(2,1)S(1)}, bf16[2048,256]{1,0:T(8,128)(2,1)}, u32[]{:S(2)}) copy-start(bf16[2048,256]{1,0:T(8,128)(2,1)} %cov_hbm.1) | copy-start | bytes 3145732
  3.5 1.0 copy-start.2
  4.5 1.0 copy-start.3
  5.5 0.9 copy-start.4
  6.5 0.7 copy-start.5
  7.2 0.7 copy-start.6
  7.9 0.7 copy-start.7
  8.6 0.7 copy-start.8
  9.3 0.7 copy-start.9
  9.9 0.7 copy-start.10
  10.6 0.7 copy-start.11

commit v2 on v1

v2 whole, which is shorter than its diff:
```python
import functools

import jax
import jax.numpy as jnp
from jax import lax
from jax.experimental import pallas as pl
from jax.experimental.pallas import tpu as pltpu
from jax.sharding import PartitionSpec as P

NB_DEV = 8
BLOCK = 128
HALO_B = 2
T_DEV = 4
PROBES = 64
NCOV = 256
OBS_DEV = 2048
ITERS = 4
NODES_DEV = 1024
COLS = T_DEV * PROBES
WIDTH = (NB_DEV + 2 * HALO_B) * BLOCK
HALO_ROWS = HALO_B * BLOCK
ROWS = NCOV + 16
EXCHANGES = ITERS + 1
CHUNK = 256
CHUNKS = NODES_DEV // CHUNK

RELAX = 0.6
MESH = pl.DeviceIdType.MESH
F32 = jnp.float32
BF16 = jnp.bfloat16
NT_DIMS = (((1,), (1,)), ((), ()))


def dot(a, b):
    return jnp.dot(a, b, preferred_element_type=F32)


def iota(shape, dim):
    return lax.broadcasted_iota(jnp.int32, shape, dim)


def mark(condition):
    return jnp.where(condition, 1.0, 0.0).astype(BF16)


def split3(values):
    first = jnp.clip(values, -3.38e38, 3.38e38).astype(BF16)
    rest = values - first.astype(F32)
    second = rest.astype(BF16)
    third = (rest - second.astype(F32)).astype(BF16)
    return first, second, third


def kernel(
    peers,
    slabs,
    cap,
    probe_hbm,
    kappa_hbm,
    theta_space_hbm,
    theta_time_hbm,
    diag_hbm,
    off_hbm,
    cols_hbm,
    needs_hbm,
    cov_hbm,
    owner_hbm,
    cell_hbm,
    coef_hbm,
    sol_ref,
    grads_ref,
    probe,
    kappa,
    theta_space,
    theta_time,
    diag,
    off,
    cols,
    needs,
    cov,
    owner,
    cell,
    coef,
    slots,
    covt,
    onehot,
    send_obs,
    recv_obs,
    masks,
    counted,
    comb,
    field,
    first_low,
    first_high,
    time_low,
    time_high,
    send_up,
    send_down,
    send_left,
    send_right,
    product,
    residual,
    edges_out,
    edges_in,
    cross_out,
    cross_in,
    local_diag,
    step,
    needs_out,
    needs_in,
    picks,
    grads_out,
    grads_in,
    load_sem,
    obs_send_sem,
    obs_recv_sem,
    needs_send_sem,
    needs_recv_sem,
    space_send_sem,
    space_recv_sem,
    time_send_sem,
    time_recv_sem,
    edges_send_sem,
    edges_recv_sem,
    cross_send_sem,
    cross_recv_sem,
    grads_send_sem,
    grads_recv_sem,
):
    me = lax.axis_index("space")
    slab = lax.axis_index("tm")
    left = lax.rem(slab + slabs - 1, slabs)
    right = lax.rem(slab + 1, slabs)
    down = lax.rem(me + peers - 1, peers)
    up = lax.rem(me + 1, peers)
    has_down, has_up = me > 0, me < peers - 1
    has_left, has_right = slab > 0, slab < slabs - 1

    pairs = (
        (owner_hbm, owner),
        (cov_hbm, cov),
        (cell_hbm, cell),
        (needs_hbm, needs),
        (probe_hbm, probe),
        (kappa_hbm, kappa),
        (theta_space_hbm, theta_space),
        (theta_time_hbm, theta_time),
        (diag_hbm, diag),
        (off_hbm, off),
        (cols_hbm, cols),
        (coef_hbm, coef),
    )
    loads = [
        pltpu.make_async_copy(src, dst, load_sem.at[i]) for i, (src, dst) in enumerate(pairs)
    ]
    for load in loads:
        load.start()

    barrier = pltpu.get_barrier_semaphore()

    def greet(k, carry):
        pl.semaphore_signal(
            barrier, inc=1, device_id=(lax.rem(me + k, peers), slab), device_id_type=MESH
        )
        return carry

    lax.fori_loop(1, peers, greet, 0)
    for other in (left, right):
        pl.semaphore_signal(barrier, inc=1, device_id=(me, other), device_id_type=MESH)

    loads[0].wait()
    owner_cols = jnp.transpose(owner[...].astype(F32))
    lanes = iota((BLOCK, BLOCK), 1)
    below = mark(iota((BLOCK, BLOCK), 1) < iota((BLOCK, BLOCK), 0))
    seen = jnp.zeros((1, BLOCK), F32)
    for c in range(OBS_DEV // BLOCK):
        owner_col = owner_cols[:, c : c + 1].astype(jnp.int32)
        hit = owner_col == lanes
        hits = mark(hit)
        before = dot(below, hits) + seen
        rank = jnp.sum(jnp.where(hit, before, 0.0), axis=1, keepdims=True)
        seen = seen + jnp.sum(hits.astype(F32), axis=0, keepdims=True)
        slot = owner_col * cap + rank.astype(jnp.int32)
        slots[c * BLOCK : (c + 1) * BLOCK, :] = jnp.broadcast_to(slot, (BLOCK, BLOCK))

    loads[1].wait()
    loads[2].wait()
    sub = iota((16, BLOCK), 0)
    for c in range(OBS_DEV // BLOCK):
        part = slice(c * BLOCK, (c + 1) * BLOCK)
        covt[:NCOV, part] = jnp.transpose(cov[part, :])
        row = jnp.broadcast_to(cell[c : c + 1, :], (16, BLOCK))
        extra = jnp.where(
            sub == 0, row // 64, jnp.where(sub == 1, row % 64, jnp.where(sub == 2, 1, 0))
        )
        covt[NCOV:, part] = extra.astype(F32).astype(BF16)

    def compact(target):
        for c in range(OBS_DEV // BLOCK):
            part = slice(c * BLOCK, (c + 1) * BLOCK)
            place = slots[part, :] - target * cap
            for h in range(0, cap, BLOCK):
                onehot[part, h : h + BLOCK] = mark(place == lanes + h)
        return dot(covt[...], onehot[...]).astype(BF16)

    pl.semaphore_wait(barrier, peers + 1)

    loads[3].wait()
    sub8 = iota((8, COLS), 0)
    listed = jnp.zeros((8, COLS), jnp.int32)
    for i in range(2 * HALO_B):
        listed = jnp.where(sub8 == i, needs[i], listed)
    needs_out[...] = listed

    def needs_copy(side, target):
        return pltpu.make_async_remote_copy(
            src_ref=needs_out,
            dst_ref=needs_in.at[side],
            send_sem=needs_send_sem.at[side],
            recv_sem=needs_recv_sem.at[side],
            device_id=(target, slab),
            device_id_type=MESH,
        )

    needs_copies = (needs_copy(0, up), needs_copy(1, down))
    for copy in needs_copies:
        copy.start()

    for i in range(4, 9):
        loads[i].wait()
    sub_e = iota((8, BLOCK), 0)
    ends = (theta_space[T_DEV - 1], theta_time[T_DEV - 1], theta_space[0], theta_time[0])
    scales = jnp.ones((8, BLOCK), F32)
    for i, value in enumerate(ends):
        scales = jnp.where(sub_e == i, value, scales)
    edges_out[...] = scales

    def beside(sends, receives, src, dst, send_sem, recv_sem, target):
        copy = pltpu.make_async_remote_copy(
            src_ref=src,
            dst_ref=dst,
            send_sem=send_sem,
            recv_sem=recv_sem,
            device_id=(me, target),
            device_id_type=MESH,
        )
        return sends, receives, copy

    def both_ways(src_right, src_left, dst_low, dst_high, send_sems, recv_sems):
        return (
            beside(has_right, has_left, src_right, dst_low, send_sems[0], recv_sems[0], right),
            beside(has_left, has_right, src_left, dst_high, send_sems[1], recv_sems[1], left),
        )

    def pair(sems, *index):
        return [sems.at[*index, which] for which in range(2)]

    edge_copies = both_ways(
        edges_out, edges_out, edges_in.at[0], edges_in.at[1], pair(edges_send_sem), pair(edges_recv_sem)
    )

    def start_copies(copies):
        for sends, _, copy in copies:
            pl.when(sends)(copy.start)

    def wait_arrivals(copies):
        for _, receives, copy in copies:
            pl.when(receives)(copy.wait_recv)

    def wait_departures(copies):
        for sends, _, copy in copies:
            pl.when(sends)(copy.wait_send)

    start_copies(edge_copies)

    def obs_copy(k, target):
        return pltpu.make_async_remote_copy(
            src_ref=send_obs.at[k],
            dst_ref=recv_obs.at[k],
            send_sem=obs_send_sem.at[k],
            recv_sem=obs_recv_sem.at[k],
            device_id=(target, slab),
            device_id_type=MESH,
        )

    def send(k, carry):
        target = lax.rem(me + k, peers)
        send_obs[k] = compact(target)
        obs_copy(k, target).start()
        return carry

    lax.fori_loop(1, peers, send, 0)
    recv_obs[0] = compact(me)

    col_time = iota((1, COLS), 1) // PROBES
    scale_space = jnp.zeros((1, COLS), F32)
    scale_time = jnp.zeros((1, COLS), F32)
    for t in range(T_DEV):
        scale_space = jnp.where(col_time == t, theta_space[t], scale_space)
        scale_time = jnp.where(col_time == t, theta_time[t], scale_time)
    kappa_cols = jnp.transpose(kappa[...])
    eye = iota((BLOCK, BLOCK), 0) == iota((BLOCK, BLOCK), 1)
    sdiag_cols = []
    for b in range(NB_DEV):
        part = slice(b * BLOCK, (b + 1) * BLOCK)
        sdiag = jnp.sum(jnp.where(eye, diag[b].astype(F32), 0.0), axis=1, keepdims=True)
        sdiag_cols.append(sdiag)
        kappa_col = kappa_cols[:, b : b + 1]
        base = scale_space * sdiag + 2.0 * scale_time + kappa_col
        step[part, :] = base
        local_diag[part, :] = jnp.broadcast_to(kappa_col, (BLOCK, COLS))
        start = RELAX * probe[part, :].astype(F32) / base
        sol_ref[part, :] = start
        field[0, part, :] = start.astype(BF16)

    for e in range(EXCHANGES):

        @pl.when(jnp.logical_not(has_down))
        def _():
            field[e, NODES_DEV : NODES_DEV + HALO_ROWS, :] = jnp.zeros((HALO_ROWS, COLS), BF16)

        @pl.when(jnp.logical_not(has_up))
        def _():
            field[e, NODES_DEV + HALO_ROWS :, :] = jnp.zeros((HALO_ROWS, COLS), BF16)

    for there, side, first, later in ((has_left, 0, first_low, time_low), (has_right, 1, first_high, time_high)):

        @pl.when(jnp.logical_not(there))
        def _():
            first[...] = jnp.zeros_like(first)
            later[...] = jnp.zeros_like(later)
            edges_in[side] = jnp.ones((8, BLOCK), F32)
            cross_in[side] = jnp.zeros((8, BLOCK), F32)

    for copy in needs_copies:
        copy.wait()
    for i in range(HALO_B):
        for b in range(NB_DEV):
            for side, row in ((1, i), (0, HALO_B + i)):
                picks[side, i, b] = mark(needs_in[side, row : row + 1, :] == b)

    lower_half = lanes < PROBES

    def pack_last(values):
        return jnp.where(
            lower_half, pltpu.roll(values[:BLOCK, BLOCK:], PROBES, 1), values[BLOCK:, BLOCK:]
        )

    def pack_first(values):
        return jnp.where(
            lower_half, values[:BLOCK, :BLOCK], pltpu.roll(values[BLOCK:, :BLOCK], PROBES, 1)
        )

    def time_copies(e, c):
        lows, highs = (first_low, first_high) if e == 0 else (time_low.at[e], time_high.at[e])
        return both_ways(
            send_right.at[e, c],
            send_left.at[e, c],
            lows.at[c],
            highs.at[c],
            pair(time_send_sem, e, c),
            pair(time_recv_sem, e, c),
        )

    def start_time(e, c, values):
        send_right[e, c] = pack_last(values).astype(BF16)
        send_left[e, c] = pack_first(values).astype(BF16)
        start_copies(time_copies(e, c))

    def space_copies(e):
        copies = []
        for which, sends, receives, src, offset, target in (
            (0, has_up, has_down, send_up, 0, up),
            (1, has_down, has_up, send_down, HALO_ROWS, down),
        ):
            copy = pltpu.make_async_remote_copy(
                src_ref=src.at[e],
                dst_ref=field.at[e, pl.ds(NODES_DEV + offset, HALO_ROWS)],
                send_sem=space_send_sem.at[e, which],
                recv_sem=space_recv_sem.at[e, which],
                device_id=(target, slab),
                device_id_type=MESH,
            )
            copies.append((sends, receives, copy))
        return copies

    def start_space(e):
        for i in range(HALO_B):
            part = slice(i * BLOCK, (i + 1) * BLOCK)
            for side, staged in ((1, send_up), (0, send_down)):
                chosen = picks[side, i, 0] * field[e, :BLOCK, :]
                for b in range(1, NB_DEV):
                    chosen = chosen + picks[side, i, b] * field[e, b * BLOCK : (b + 1) * BLOCK, :]
                staged[e, part, :] = chosen
        start_copies(space_copies(e))

    start_space(0)
    for c in range(CHUNKS):
        start_time(0, c, probe[c * CHUNK : (c + 1) * CHUNK, :].astype(F32))

    loads[9].wait()
    loads[10].wait()

    def combine(i, carry):
        b = i // NB_DEV
        rows = pl.ds(pl.multiple_of((i % NB_DEV) * 16, 16), 16)
        parts = [off[b, k, rows, :].astype(F32) for k in range(NB_DEV)]
        own = diag[b, rows, :].astype(F32)
        columns = [cols[b, k] for k in range(NB_DEV)]
        place = pl.ds(pl.multiple_of(i * 16, 16), 16)
        for m in range(WIDTH // BLOCK):
            total = jnp.zeros((16, BLOCK), F32)
            for k in range(NB_DEV):
                total = total + jnp.where(columns[k] == m, 1.0, 0.0) * parts[k]
            if m < NB_DEV:
                total = total + jnp.where(b == m, 1.0, 0.0) * own
            comb[place, m * BLOCK : (m + 1) * BLOCK] = total.astype(BF16)
        return carry

    lax.fori_loop(0, NODES_DEV // 16, combine, 0)

    row_t, lane_t = iota((COLS, COLS), 0), iota((COLS, COLS), 1)
    inner = jnp.where(
        row_t == lane_t, 2.0, jnp.where(jnp.abs(row_t - lane_t) == PROBES, -1.0, 0.0)
    ).astype(BF16)
    def own_product(e):
        product[...] = dot(comb[:, :NODES_DEV], field[e, :NODES_DEV, :])

    def both(e, part):
        space = product[part, :] + dot(comb[part, NODES_DEV:], field[e, NODES_DEV:, :])
        return space, dot(field[e, part, :], inner)

    def parts():
        for c in range(CHUNKS):
            yield c, slice(c * CHUNK, (c + 1) * CHUNK)

    def inner_residual(e):
        for _, part in parts():
            space, time = both(e, part)
            applied = (
                scale_space * space
                + scale_time * time
                + local_diag[part, :] * field[e, part, :].astype(F32)
            )
            residual[part, :] = probe[part, :].astype(F32) - applied

    def update(e, c, part):
        low, high = time_low[e, c].astype(F32), time_high[e, c].astype(F32)
        first = scale_time[:, :BLOCK] * jnp.concatenate(
            [jnp.where(lower_half, low, 0.0), jnp.where(lower_half, pltpu.roll(low, PROBES, 1), 0.0)], axis=0
        )
        last = scale_time[:, BLOCK:] * jnp.concatenate(
            [jnp.where(lower_half, 0.0, pltpu.roll(high, PROBES, 1)), jnp.where(lower_half, 0.0, high)], axis=0
        )
        left_over = residual[part, :] + jnp.concatenate([first, last], axis=1)
        solved = sol_ref[part, :] + step[part, :] * left_over
        sol_ref[part, :] = solved
        field[e + 1, part, :] = solved.astype(BF16)
        return solved

    own_product(0)

    loads[11].wait()
    counted[...] = jnp.zeros((NODES_DEV, BLOCK), F32)
    row_w = iota((BLOCK, cap), 0)

    def weigh(k):
        digits = recv_obs[k, NCOV:, :].astype(F32)
        live = digits[2:3, :] > 0.5
        number = (digits[0:1, :] * 64.0 + digits[1:2, :]).astype(jnp.int32)
        node = jnp.where(live, number // T_DEV, -1)
        time = number % T_DEV
        rows = recv_obs[k, :NCOV, :]
        eta = jnp.zeros((1, cap), F32)
        for c in range(NODES_DEV // CHUNK):
            part = slice(c * CHUNK, (c + 1) * CHUNK)
            scores = dot(coef[part, :], rows)
            found = iota((CHUNK, cap), 0) + c * CHUNK == node
            eta = eta + jnp.sum(jnp.where(found, scores, 0.0), axis=0, keepdims=True)
            masks[part, :] = mark(found)
        weight = jnp.where(live, jnp.exp(eta), 0.0)
        pieces = [piece.astype(F32) for piece in split3(weight)]
        spread = jnp.zeros((BLOCK, cap), F32)
        for i, piece in enumerate(pieces):
            spread = jnp.where(row_w == time + i * T_DEV, piece, spread)
        counted[...] += lax.dot_general(
            masks[...], spread.astype(BF16), NT_DIMS, preferred_element_type=F32
        )

    weigh(0)

    def receive(k, carry):
        obs_copy(k, lax.rem(me + k, peers)).wait_recv()
        weigh(k)
        return carry

    lax.fori_loop(1, peers, receive, 0)

    spread_row, spread_col = iota((BLOCK, COLS), 0), iota((BLOCK, COLS), 1) // PROBES
    repeat = mark((spread_row < 3 * T_DEV) & (spread_row % T_DEV == spread_col))
    for _, part in parts():
        pieces = split3(counted[part, :])
        obs_diag = dot(pieces[0], repeat) + dot(pieces[1], repeat) + dot(pieces[2], repeat)
        local_diag[part, :] = local_diag[part, :] + obs_diag
        step[part, :] = RELAX / (step[part, :] + obs_diag)

    wait_arrivals(edge_copies)
    for c in range(CHUNKS):
        wait_arrivals(time_copies(0, c))
        lo, hi = 2 * c, 2 * c + 1
        sdiag = jnp.where(lower_half, sdiag_cols[lo], sdiag_cols[hi])
        nugget = jnp.where(lower_half, kappa_cols[:, lo : lo + 1], kappa_cols[:, hi : hi + 1])
        for side, row, first, later in ((0, 0, first_low, time_low), (1, 2, first_high, time_high)):
            base = edges_in[side, row : row + 1, :] * sdiag + 2.0 * edges_in[side, row + 1 : row + 2, :] + nugget
            later[0, c] = (RELAX * first[c].astype(F32) / base).astype(BF16)

    crossed = [jnp.zeros((1, BLOCK), F32), jnp.zeros((1, BLOCK), F32)]
    for e in range(ITERS):
        wait_arrivals(space_copies(e))
        inner_residual(e)
        for c, part in parts():
            if e > 0:
                wait_arrivals(time_copies(e, c))
            solved = update(e, c, part)
            if e < ITERS - 1:
                start_time(e + 1, c, solved)
            else:
                rounded = solved.astype(BF16).astype(F32)
                for i, packed, there in ((0, pack_last(rounded), first_high), (1, pack_first(rounded), first_low)):
                    terms = packed * there[c].astype(F32)
                    crossed[i] = crossed[i] + jnp.sum(terms, axis=0, keepdims=True)
        start_space(e + 1)
        if e < ITERS - 1:
            own_product(e + 1)

    for i in range(2):
        cross_out[i] = jnp.broadcast_to(crossed[i], (8, BLOCK))
    cross_copies = both_ways(
        cross_out.at[0],
        cross_out.at[1],
        cross_in.at[0],
        cross_in.at[1],
        pair(cross_send_sem),
        pair(cross_recv_sem),
    )
    start_copies(cross_copies)
    own_product(ITERS)
    wait_arrivals(space_copies(ITERS))
    sums = [jnp.zeros((1, COLS), F32), jnp.zeros((1, COLS), F32)]
    for _, part in parts():
        values = probe[part, :].astype(F32)
        for i, term in enumerate(both(ITERS, part)):
            sums[i] = sums[i] + jnp.sum(values * term, axis=0, keepdims=True)
    wait_arrivals(cross_copies)
    folded = [cross_in[i] + pltpu.roll(cross_in[i], PROBES, 1) for i in range(2)]
    low8 = iota((8, BLOCK), 1) < PROBES
    owed = jnp.concatenate([jnp.where(low8, folded[0], 0.0), jnp.where(low8, 0.0, folded[1])], axis=1)
    sums[1] = sums[1] - owed[0:1, :]
    grads_out[...] = jnp.where(sub8 == 0, sums[0], jnp.where(sub8 == 1, sums[1], 0.0))
    grads_in[me] = grads_out[...]

    def grads_copy(k):
        target = lax.rem(me + k, peers)
        return pltpu.make_async_remote_copy(
            src_ref=grads_out,
            dst_ref=grads_in.at[me],
            send_sem=grads_send_sem.at[k],
            recv_sem=grads_recv_sem.at[k],
            device_id=(target, slab),
            device_id_type=MESH,
        )

    def grads_send(k, carry):
        grads_copy(k).start()
        return carry

    lax.fori_loop(1, peers, grads_send, 0)

    def finish(k, carry):
        grads_copy(k).wait()
        obs_copy(k, lax.rem(me + k, peers)).wait_send()
        return carry

    lax.fori_loop(1, peers, finish, 0)
    wait_departures(edge_copies)
    wait_departures(cross_copies)
    for e in range(EXCHANGES):
        wait_departures(space_copies(e))
        if e < ITERS:
            for c in range(CHUNKS):
                wait_departures(time_copies(e, c))
    total = grads_in[0]
    for s in range(1, peers):
        total = total + grads_in[s]
    grads_ref[...] = total[0:2, :] / (NODES_DEV * peers)


def shards(
    probe_field,
    kappa,
    theta_space,
    theta_time,
    diag_blocks,
    off_blocks,
    block_cols,
    halo_needs,
    covariates,
    obs_owner,
    obs_cell,
    svc_coef,
):
    peers = lax.axis_size("space")
    slabs = lax.axis_size("tm")
    cap = 2 * OBS_DEV // peers
    vmem = pl.BlockSpec(memory_space=pltpu.VMEM)
    dma = pltpu.SemaphoreType.DMA
    return pl.pallas_call(
        functools.partial(kernel, peers, slabs, cap),
        out_shape=(
            jax.ShapeDtypeStruct((NODES_DEV, COLS), F32),
            jax.ShapeDtypeStruct((2, COLS), F32),
        ),
        in_specs=[pl.BlockSpec(memory_space=pltpu.HBM)] * 12,
        out_specs=(vmem, vmem),
        scratch_shapes=[
            pltpu.VMEM((NODES_DEV, COLS), BF16),
            pltpu.VMEM((NB_DEV, BLOCK), F32),
            pltpu.SMEM((T_DEV,), F32),
            pltpu.SMEM((T_DEV,), F32),
            pltpu.VMEM((NB_DEV, BLOCK, BLOCK), BF16),
            pltpu.VMEM((NB_DEV, NB_DEV, BLOCK, BLOCK), BF16),
            pltpu.SMEM((NB_DEV, NB_DEV), jnp.int32),
            pltpu.SMEM((2 * HALO_B,), jnp.int32),
            pltpu.VMEM((OBS_DEV, NCOV), BF16),
            pltpu.VMEM((OBS_DEV // BLOCK, BLOCK), jnp.int32),
            pltpu.VMEM((OBS_DEV // BLOCK, BLOCK), jnp.int32),
            pltpu.VMEM((NODES_DEV, NCOV), BF16),
            pltpu.VMEM((OBS_DEV, BLOCK), jnp.int32),
            pltpu.VMEM((ROWS, OBS_DEV), BF16),
            pltpu.VMEM((OBS_DEV, cap), BF16),
            pltpu.VMEM((peers, ROWS, cap), BF16),
            pltpu.VMEM((peers, ROWS, cap), BF16),
            pltpu.VMEM((NODES_DEV, cap), BF16),
            pltpu.VMEM((NODES_DEV, BLOCK), F32),
            pltpu.VMEM((NODES_DEV, WIDTH), BF16),
            pltpu.VMEM((EXCHANGES, WIDTH, COLS), BF16),
            pltpu.VMEM((CHUNKS, BLOCK, BLOCK), BF16),
            pltpu.VMEM((CHUNKS, BLOCK, BLOCK), BF16),
            pltpu.VMEM((ITERS, CHUNKS, BLOCK, BLOCK), BF16),
            pltpu.VMEM((ITERS, CHUNKS, BLOCK, BLOCK), BF16),
            pltpu.VMEM((EXCHANGES, HALO_ROWS, COLS), BF16),
            pltpu.VMEM((EXCHANGES, HALO_ROWS, COLS), BF16),
            pltpu.VMEM((ITERS, CHUNKS, BLOCK, BLOCK), BF16),
            pltpu.VMEM((ITERS, CHUNKS, BLOCK, BLOCK), BF16),
            pltpu.VMEM((NODES_DEV, COLS), F32),
            pltpu.VMEM((NODES_DEV, COLS), F32),
            pltpu.VMEM((8, BLOCK), F32),
            pltpu.VMEM((2, 8, BLOCK), F32),
            pltpu.VMEM((2, 8, BLOCK), F32),
            pltpu.VMEM((2, 8, BLOCK), F32),
            pltpu.VMEM((NODES_DEV, COLS), F32),
            pltpu.VMEM((NODES_DEV, COLS), F32),
            pltpu.VMEM((8, COLS), jnp.int32),
            pltpu.VMEM((2, 8, COLS), jnp.int32),
            pltpu.VMEM((2, HALO_B, NB_DEV, 1, COLS), BF16),
            pltpu.VMEM((8, COLS), F32),
            pltpu.VMEM((peers, 8, COLS), F32),
            dma((12,)),
            dma((peers,)),
            dma((peers,)),
            dma((2,)),
            dma((2,)),
            dma((EXCHANGES, 2)),
            dma((EXCHANGES, 2)),
            dma((ITERS, CHUNKS, 2)),
            dma((ITERS, CHUNKS, 2)),
            dma((2,)),
            dma((2,)),
            dma((2,)),
            dma((2,)),
            dma((peers,)),
            dma((peers,)),
        ],
        compiler_params=pltpu.CompilerParams(
            collective_id=0,
            has_side_effects=True,
            vmem_limit_bytes=60 * 1024 * 1024,
        ),
    )(
        probe_field,
        kappa.reshape(NB_DEV, BLOCK),
        theta_space,
        theta_time,
        diag_blocks,
        off_blocks,
        block_cols,
        halo_needs,
        covariates,
        obs_owner.reshape(OBS_DEV // BLOCK, BLOCK),
        obs_cell.reshape(OBS_DEV // BLOCK, BLOCK),
        svc_coef,
    )


def solution(mesh):
    return jax.shard_map(
        shards,
        mesh=mesh,
        in_specs=(
            P("space", "tm"),
            P("space"),
            P("tm"),
            P("tm"),
            P("space", None, None),
            P("space", None, None, None),
            P("space", None),
            P("space"),
            P(("space", "tm"), None),
            P(("space", "tm"), None),
            P(("space", "tm")),
            P("space", None),
        ),
        out_specs=(P("space", "tm"), P(None, "tm")),
        check_vma=False,
    )
```

time: 110 us -> 95.6 us (0.87)
  local copies, waits for them, and re-layouts: 12.1 us -> 2.84 us
  Pallas kernels: 96.9 us -> 91.5 us
    unnamed x26 -> x4, local copies, waits for them, and re-layouts: 12.1 us -> 2.84 us
    pallas_call x1, Pallas kernels: 96.9 us -> 91.5 us  [shards(): pl.pallas_call(functools.partial(kernel, peers, slabs, cap), out_shape=(j...]
where the time goes in v2:
time: 95.6 us; the launch traced here: 95 us
  Pallas kernels  91.5 us (96%)
  local copies, waits for them, and re-layouts  2.84 us (3%)
    pallas_call x1, Pallas kernels, shards(): pl.pallas_call(functools.partial(kernel, peers, slabs, cap), out_shape=(j...  91.5 us
    unnamed x4, local copies, waits for them, and re-layouts  2.84 us

profile of v2, /device:TPU:5, one launch (start us, length us, event | category | flops | bytes accessed | tf_op | source)
XLA Modules:
  0.0 95.0 jit_solution(2701846463199101690)
XLA Ops:
  0.6 91.5 %shard_map.131 = (f32[1024,256]{1,0:T(8,128)}, f32[2,256]{1,0:T(2,128)}) custom-call(bf16[1024,256]{1,0:T(8,128)(2,1)} %probe_hbm.1, f32[8,128]{1,0:T(8,128)} %bitcast.5, f32[4]{0:T(128)} %theta_space_hbm.1, f32[4]{0:T(128)} %theta_time_hbm.1, bf16[8,128,128]{2,1,0:T(8,128)(2,1)} %diag_hbm.1, bf16[8,8,128,128]{3,2,1,0:T(8,128)(2,1)} %off_hbm.1, ...), custom_call_target="tpu_custom_call" | custom-call | tf_op jit(solution)/shard_map/pallas_call | solution.py:617
  92.1 0.0 copy-start
  92.1 2.3 %copy.16 = f32[1024,256]{1,0:T(8,128)} copy(f32[1024,256]{1,0:T(8,128)} %get-tuple-element.4) | data formatting | bytes 2097152
  94.4 0.0 copy-done
  94.4 0.6 copy.17
Async XLA Ops:
  92.1 2.3 %copy-start = (f32[2,256]{1,0:T(2,128)S(1)}, f32[2,256]{1,0:T(2,128)}, u32[]{:S(2)}) copy-start(f32[2,256]{1,0:T(2,128)} %get-tuple-element.5) | copy-start | bytes 6148

commit v3 on v2

--- a/solution.py
+++ b/solution.py
@@ -23,6 +23,10 @@
 EXCHANGES = ITERS + 1
 CHUNK = 256
 CHUNKS = NODES_DEV // CHUNK
+GROUP = 4
+THIN = PROBES // GROUP
+HALF = NODES_DEV // 2
+CELLS = NB_DEV * T_DEV
 
 RELAX = 0.6
 MESH = pl.DeviceIdType.MESH
@@ -90,8 +94,6 @@
     counted,
     comb,
     field,
-    first_low,
-    first_high,
     time_low,
     time_high,
     send_up,
@@ -100,15 +102,23 @@
     send_right,
     product,
     residual,
-    edges_out,
-    edges_in,
-    cross_out,
-    cross_in,
-    local_diag,
-    step,
+    fine,
+    turned,
+    swap_out,
+    swap_in,
+    back_out,
+    back_in,
+    scales_out,
+    scales_in,
+    sums_out,
+    sums_in,
     needs_out,
     needs_in,
     picks,
+    local_diag,
+    step,
+    run_out,
+    run_in,
     grads_out,
     grads_in,
     load_sem,
@@ -120,21 +130,29 @@
     space_recv_sem,
     time_send_sem,
     time_recv_sem,
-    edges_send_sem,
-    edges_recv_sem,
-    cross_send_sem,
-    cross_recv_sem,
+    swap_send_sem,
+    swap_recv_sem,
+    back_send_sem,
+    back_recv_sem,
+    scales_send_sem,
+    scales_recv_sem,
+    sums_send_sem,
+    sums_recv_sem,
+    run_send_sem,
+    run_recv_sem,
     grads_send_sem,
     grads_recv_sem,
 ):
     me = lax.axis_index("space")
     slab = lax.axis_index("tm")
-    left = lax.rem(slab + slabs - 1, slabs)
-    right = lax.rem(slab + 1, slabs)
+    turn = lax.rem(slab, GROUP)
+    run = slab - turn
+    left = lax.rem(slab + slabs - GROUP, slabs)
+    right = lax.rem(slab + GROUP, slabs)
     down = lax.rem(me + peers - 1, peers)
     up = lax.rem(me + 1, peers)
     has_down, has_up = me > 0, me < peers - 1
-    has_left, has_right = slab > 0, slab < slabs - 1
+    has_left, has_right = run > 0, run < slabs - GROUP
 
     pairs = (
         (owner_hbm, owner),
@@ -165,7 +183,9 @@
         return carry
 
     lax.fori_loop(1, peers, greet, 0)
-    for other in (left, right):
+    ahead = [run + lax.rem(turn + k, GROUP) for k in range(GROUP)]
+    behind = [lax.rem(turn + GROUP - k, GROUP) for k in range(GROUP)]
+    for other in (left, right, *ahead[1:]):
         pl.semaphore_signal(barrier, inc=1, device_id=(me, other), device_id_type=MESH)
 
     loads[0].wait()
@@ -203,7 +223,7 @@
                 onehot[part, h : h + BLOCK] = mark(place == lanes + h)
         return dot(covt[...], onehot[...]).astype(BF16)
 
-    pl.semaphore_wait(barrier, peers + 1)
+    pl.semaphore_wait(barrier, peers + GROUP)
 
     loads[3].wait()
     sub8 = iota((8, COLS), 0)
@@ -228,12 +248,67 @@
 
     for i in range(4, 9):
         loads[i].wait()
-    sub_e = iota((8, BLOCK), 0)
-    ends = (theta_space[T_DEV - 1], theta_time[T_DEV - 1], theta_space[0], theta_time[0])
-    scales = jnp.ones((8, BLOCK), F32)
-    for i, value in enumerate(ends):
-        scales = jnp.where(sub_e == i, value, scales)
-    edges_out[...] = scales
+    col = iota((8, COLS), 1)
+    sub8 = iota((8, COLS), 0)
+    mine = jnp.zeros((8, COLS), F32)
+    for t in range(T_DEV):
+        here = (col // PROBES == turn) & ((col // THIN) % T_DEV == t)
+        mine = jnp.where(here & (sub8 == 0), theta_space[t], mine)
+        mine = jnp.where(here & (sub8 == 1), theta_time[t], mine)
+    scales_out[...] = mine
+
+    def group_copy(k, src, dst, send_sem, recv_sem):
+        return pltpu.make_async_remote_copy(
+            src_ref=src,
+            dst_ref=dst,
+            send_sem=send_sem.at[k],
+            recv_sem=recv_sem.at[k],
+            device_id=(me, ahead[k]),
+            device_id_type=MESH,
+        )
+
+    scales_copies = [
+        group_copy(k, scales_out, scales_in.at[k], scales_send_sem, scales_recv_sem) for k in range(1, GROUP)
+    ]
+    swap_copies = [
+        group_copy(k, swap_out.at[k], swap_in.at[k], swap_send_sem, swap_recv_sem) for k in range(1, GROUP)
+    ]
+    back_copies = [
+        group_copy(k, back_out.at[k], back_in.at[k], back_send_sem, back_recv_sem) for k in range(1, GROUP)
+    ]
+    place = pl.ds(pl.multiple_of(turn * CELLS, CELLS), CELLS)
+    sums_copies = [
+        group_copy(k, sums_out, sums_in.at[place], sums_send_sem, sums_recv_sem) for k in range(1, GROUP)
+    ]
+
+    tall, wide = (iota((COLS, BLOCK), i) for i in range(2))
+    low_tall, high_wide = (iota((BLOCK, COLS), i) for i in range(2))
+
+    def by_probe(lane, which):
+        return (lane // THIN) * PROBES + which * THIN + lane % THIN
+
+    def by_time(lane, which):
+        return which * PROBES + lane
+
+    def take(source, order, which):
+        left_half = mark((wide < PROBES) & (tall == order(wide, which)))
+        right_half = mark((wide >= PROBES) & (tall == order(wide - PROBES, which)))
+        return (dot(source[:HALF, :], left_half) + dot(source[HALF:, :], right_half)).astype(BF16)
+
+    def put(terms, order):
+        halves = [jnp.zeros((HALF, COLS), F32), jnp.zeros((HALF, COLS), F32)]
+        for value, which in terms:
+            for half in range(2):
+                lane = low_tall - half * PROBES
+                keep = (low_tall // PROBES == half) & (high_wide == order(lane, which))
+                halves[half] = halves[half] + dot(value, mark(keep))
+        return halves
+
+    swap_in[0] = take(probe, by_probe, turn)
+    for k in range(1, GROUP):
+        swap_out[k] = take(probe, by_probe, lax.rem(turn + k, GROUP))
+    for copy in scales_copies + swap_copies:
+        copy.start()
 
     def beside(sends, receives, src, dst, send_sem, recv_sem, target):
         copy = pltpu.make_async_remote_copy(
@@ -255,10 +330,6 @@
     def pair(sems, *index):
         return [sems.at[*index, which] for which in range(2)]
 
-    edge_copies = both_ways(
-        edges_out, edges_out, edges_in.at[0], edges_in.at[1], pair(edges_send_sem), pair(edges_recv_sem)
-    )
-
     def start_copies(copies):
         for sends, _, copy in copies:
             pl.when(sends)(copy.start)
@@ -271,7 +342,6 @@
         for sends, _, copy in copies:
             pl.when(sends)(copy.wait_send)
 
-    start_copies(edge_copies)
 
     def obs_copy(k, target):
         return pltpu.make_async_remote_copy(
@@ -292,25 +362,26 @@
     lax.fori_loop(1, peers, send, 0)
     recv_obs[0] = compact(me)
 
-    col_time = iota((1, COLS), 1) // PROBES
-    scale_space = jnp.zeros((1, COLS), F32)
-    scale_time = jnp.zeros((1, COLS), F32)
-    for t in range(T_DEV):
-        scale_space = jnp.where(col_time == t, theta_space[t], scale_space)
-        scale_time = jnp.where(col_time == t, theta_time[t], scale_time)
+    total = mine
+    for k in range(1, GROUP):
+        scales_copies[k - 1].wait_recv()
+        total = total + scales_in[k]
+    scale_space, scale_time = total[0:1, :], total[1:2, :]
+    for copy in swap_copies:
+        copy.wait_recv()
+    for half, values in enumerate(put([(swap_in[k], behind[k]) for k in range(GROUP)], by_time)):
+        turned[half * HALF : (half + 1) * HALF, :] = values.astype(BF16)
     kappa_cols = jnp.transpose(kappa[...])
     eye = iota((BLOCK, BLOCK), 0) == iota((BLOCK, BLOCK), 1)
-    sdiag_cols = []
     for b in range(NB_DEV):
         part = slice(b * BLOCK, (b + 1) * BLOCK)
         sdiag = jnp.sum(jnp.where(eye, diag[b].astype(F32), 0.0), axis=1, keepdims=True)
-        sdiag_cols.append(sdiag)
         kappa_col = kappa_cols[:, b : b + 1]
         base = scale_space * sdiag + 2.0 * scale_time + kappa_col
         step[part, :] = base
         local_diag[part, :] = jnp.broadcast_to(kappa_col, (BLOCK, COLS))
-        start = RELAX * probe[part, :].astype(F32) / base
-        sol_ref[part, :] = start
+        start = RELAX * turned[part, :].astype(F32) / base
+        fine[part, :] = start
         field[0, part, :] = start.astype(BF16)
 
     for e in range(EXCHANGES):
@@ -323,14 +394,11 @@
         def _():
             field[e, NODES_DEV + HALO_ROWS :, :] = jnp.zeros((HALO_ROWS, COLS), BF16)
 
-    for there, side, first, later in ((has_left, 0, first_low, time_low), (has_right, 1, first_high, time_high)):
+    for there, later in ((has_left, time_low), (has_right, time_high)):
 
         @pl.when(jnp.logical_not(there))
         def _():
-            first[...] = jnp.zeros_like(first)
             later[...] = jnp.zeros_like(later)
-            edges_in[side] = jnp.ones((8, BLOCK), F32)
-            cross_in[side] = jnp.zeros((8, BLOCK), F32)
 
     for copy in needs_copies:
         copy.wait()
@@ -339,33 +407,28 @@
             for side, row in ((1, i), (0, HALO_B + i)):
                 picks[side, i, b] = mark(needs_in[side, row : row + 1, :] == b)
 
-    lower_half = lanes < PROBES
-
-    def pack_last(values):
-        return jnp.where(
-            lower_half, pltpu.roll(values[:BLOCK, BLOCK:], PROBES, 1), values[BLOCK:, BLOCK:]
-        )
-
-    def pack_first(values):
-        return jnp.where(
-            lower_half, values[:BLOCK, :BLOCK], pltpu.roll(values[BLOCK:, :BLOCK], PROBES, 1)
-        )
-
-    def time_copies(e, c):
-        lows, highs = (first_low, first_high) if e == 0 else (time_low.at[e], time_high.at[e])
+    def pack(e, first, shift):
+        packed = jnp.zeros((BLOCK, BLOCK), F32)
+        for b in range(NB_DEV):
+            edge = field[e, b * BLOCK : (b + 1) * BLOCK, first : first + BLOCK].astype(F32)
+            moved = pltpu.roll(edge, (shift + b * THIN) % BLOCK, 1)
+            packed = jnp.where(lanes // THIN == b, moved, packed)
+        return packed.astype(BF16)
+
+    def time_copies(e):
         return both_ways(
-            send_right.at[e, c],
-            send_left.at[e, c],
-            lows.at[c],
-            highs.at[c],
-            pair(time_send_sem, e, c),
-            pair(time_recv_sem, e, c),
-        )
-
-    def start_time(e, c, values):
-        send_right[e, c] = pack_last(values).astype(BF16)
-        send_left[e, c] = pack_first(values).astype(BF16)
-        start_copies(time_copies(e, c))
+            send_right.at[e],
+            send_left.at[e],
+            time_low.at[e],
+            time_high.at[e],
+            pair(time_send_sem, e),
+            pair(time_recv_sem, e),
+        )
+
+    def start_time(e):
+        send_right[e] = pack(e, COLS - BLOCK, THIN)
+        send_left[e] = pack(e, 0, 0)
+        start_copies(time_copies(e))
 
     def space_copies(e):
         copies = []
@@ -395,8 +458,7 @@
         start_copies(space_copies(e))
 
     start_space(0)
-    for c in range(CHUNKS):
-        start_time(0, c, probe[c * CHUNK : (c + 1) * CHUNK, :].astype(F32))
+    start_time(0)
 
     loads[9].wait()
     loads[10].wait()
@@ -421,7 +483,7 @@
 
     row_t, lane_t = iota((COLS, COLS), 0), iota((COLS, COLS), 1)
     inner = jnp.where(
-        row_t == lane_t, 2.0, jnp.where(jnp.abs(row_t - lane_t) == PROBES, -1.0, 0.0)
+        row_t == lane_t, 2.0, jnp.where(jnp.abs(row_t - lane_t) == THIN, -1.0, 0.0)
     ).astype(BF16)
     def own_product(e):
         product[...] = dot(comb[:, :NODES_DEV], field[e, :NODES_DEV, :])
@@ -434,29 +496,28 @@
         for c in range(CHUNKS):
             yield c, slice(c * CHUNK, (c + 1) * CHUNK)
 
-    def inner_residual(e):
-        for _, part in parts():
+    def beside_term(e, b):
+        low, high = time_low[e].astype(F32), time_high[e].astype(F32)
+        first = pltpu.roll(low, (BLOCK - b * THIN) % BLOCK, 1)
+        last = pltpu.roll(high, (BLOCK - THIN - b * THIN) % BLOCK, 1)
+        return jnp.concatenate(
+            [jnp.where(lanes < THIN, first, 0.0), jnp.where(lanes >= BLOCK - THIN, last, 0.0)], axis=1
+        )
+
+    def beside_terms(e, c):
+        return jnp.concatenate([beside_term(e, c * 2), beside_term(e, c * 2 + 1)], axis=0)
+
+    def sweep(e):
+        for c, part in parts():
             space, time = both(e, part)
             applied = (
                 scale_space * space
-                + scale_time * time
+                + scale_time * (time - beside_terms(e, c))
                 + local_diag[part, :] * field[e, part, :].astype(F32)
             )
-            residual[part, :] = probe[part, :].astype(F32) - applied
-
-    def update(e, c, part):
-        low, high = time_low[e, c].astype(F32), time_high[e, c].astype(F32)
-        first = scale_time[:, :BLOCK] * jnp.concatenate(
-            [jnp.where(lower_half, low, 0.0), jnp.where(lower_half, pltpu.roll(low, PROBES, 1), 0.0)], axis=0
-        )
-        last = scale_time[:, BLOCK:] * jnp.concatenate(
-            [jnp.where(lower_half, 0.0, pltpu.roll(high, PROBES, 1)), jnp.where(lower_half, 0.0, high)], axis=0
-        )
-        left_over = residual[part, :] + jnp.concatenate([first, last], axis=1)
-        solved = sol_ref[part, :] + step[part, :] * left_over
-        sol_ref[part, :] = solved
-        field[e + 1, part, :] = solved.astype(BF16)
-        return solved
+            solved = fine[part, :] + step[part, :] * (turned[part, :].astype(F32) - applied)
+            fine[part, :] = solved
+            field[e + 1, part, :] = solved.astype(BF16)
 
     own_product(0)
 
@@ -496,67 +557,68 @@
 
     lax.fori_loop(1, peers, receive, 0)
 
-    spread_row, spread_col = iota((BLOCK, COLS), 0), iota((BLOCK, COLS), 1) // PROBES
-    repeat = mark((spread_row < 3 * T_DEV) & (spread_row % T_DEV == spread_col))
-    for _, part in parts():
-        pieces = split3(counted[part, :])
+    packed = jnp.zeros((BLOCK, BLOCK), F32)
+    for b in range(NB_DEV):
+        held = counted[b * BLOCK : (b + 1) * BLOCK, :]
+        held = held + pltpu.roll(held, BLOCK - T_DEV, 1) + pltpu.roll(held, BLOCK - 2 * T_DEV, 1)
+        packed = jnp.where(lanes // T_DEV == b, pltpu.roll(held, b * T_DEV, 1), packed)
+    sums_out[...] = jnp.transpose(packed)[:CELLS, :]
+    sums_in[place, :] = sums_out[...]
+    for copy in sums_copies:
+        copy.start()
+    for copy in sums_copies:
+        copy.wait_recv()
+    pieces = split3(jnp.transpose(sums_in[...]))
+    for b in range(NB_DEV):
+        part = slice(b * BLOCK, (b + 1) * BLOCK)
+        cell_of = (high_wide // PROBES) * CELLS + b * T_DEV + (high_wide // THIN) % T_DEV
+        repeat = mark(low_tall == cell_of)
         obs_diag = dot(pieces[0], repeat) + dot(pieces[1], repeat) + dot(pieces[2], repeat)
         local_diag[part, :] = local_diag[part, :] + obs_diag
         step[part, :] = RELAX / (step[part, :] + obs_diag)
 
-    wait_arrivals(edge_copies)
-    for c in range(CHUNKS):
-        wait_arrivals(time_copies(0, c))
-        lo, hi = 2 * c, 2 * c + 1
-        sdiag = jnp.where(lower_half, sdiag_cols[lo], sdiag_cols[hi])
-        nugget = jnp.where(lower_half, kappa_cols[:, lo : lo + 1], kappa_cols[:, hi : hi + 1])
-        for side, row, first, later in ((0, 0, first_low, time_low), (1, 2, first_high, time_high)):
-            base = edges_in[side, row : row + 1, :] * sdiag + 2.0 * edges_in[side, row + 1 : row + 2, :] + nugget
-            later[0, c] = (RELAX * first[c].astype(F32) / base).astype(BF16)
-
-    crossed = [jnp.zeros((1, BLOCK), F32), jnp.zeros((1, BLOCK), F32)]
     for e in range(ITERS):
         wait_arrivals(space_copies(e))
-        inner_residual(e)
-        for c, part in parts():
-            if e > 0:
-                wait_arrivals(time_copies(e, c))
-            solved = update(e, c, part)
-            if e < ITERS - 1:
-                start_time(e + 1, c, solved)
-            else:
-                rounded = solved.astype(BF16).astype(F32)
-                for i, packed, there in ((0, pack_last(rounded), first_high), (1, pack_first(rounded), first_low)):
-                    terms = packed * there[c].astype(F32)
-                    crossed[i] = crossed[i] + jnp.sum(terms, axis=0, keepdims=True)
+        wait_arrivals(time_copies(e))
+        sweep(e)
         start_space(e + 1)
+        start_time(e + 1)
         if e < ITERS - 1:
             own_product(e + 1)
 
-    for i in range(2):
-        cross_out[i] = jnp.broadcast_to(crossed[i], (8, BLOCK))
-    cross_copies = both_ways(
-        cross_out.at[0],
-        cross_out.at[1],
-        cross_in.at[0],
-        cross_in.at[1],
-        pair(cross_send_sem),
-        pair(cross_recv_sem),
-    )
-    start_copies(cross_copies)
+    for k in range(1, GROUP):
+        back_out[k] = take(field.at[ITERS, pl.ds(0, NODES_DEV)], by_time, lax.rem(turn + k, GROUP))
+        back_copies[k - 1].start()
     own_product(ITERS)
+    kept = take(field.at[ITERS, pl.ds(0, NODES_DEV)], by_time, turn)
+    for _, part in parts():
+        rest = fine[part, :] - field[ITERS, part, :].astype(F32)
+        residual[part, :] = rest.astype(BF16)
+    small = take(residual, by_time, turn)
     wait_arrivals(space_copies(ITERS))
+    wait_arrivals(time_copies(ITERS))
     sums = [jnp.zeros((1, COLS), F32), jnp.zeros((1, COLS), F32)]
-    for _, part in parts():
-        values = probe[part, :].astype(F32)
-        for i, term in enumerate(both(ITERS, part)):
+    for c, part in parts():
+        values = turned[part, :].astype(F32)
+        space, time = both(ITERS, part)
+        for i, term in enumerate((space, time - beside_terms(ITERS, c))):
             sums[i] = sums[i] + jnp.sum(values * term, axis=0, keepdims=True)
-    wait_arrivals(cross_copies)
-    folded = [cross_in[i] + pltpu.roll(cross_in[i], PROBES, 1) for i in range(2)]
-    low8 = iota((8, BLOCK), 1) < PROBES
-    owed = jnp.concatenate([jnp.where(low8, folded[0], 0.0), jnp.where(low8, 0.0, folded[1])], axis=1)
-    sums[1] = sums[1] - owed[0:1, :]
-    grads_out[...] = jnp.where(sub8 == 0, sums[0], jnp.where(sub8 == 1, sums[1], 0.0))
+    run_out[...] = jnp.where(sub8 == 0, sums[0], jnp.where(sub8 == 1, sums[1], 0.0))
+    run_in[0] = run_out[...]
+    run_copies = [
+        group_copy(k, run_out, run_in.at[k], run_send_sem, run_recv_sem) for k in range(1, GROUP)
+    ]
+    for copy in run_copies:
+        copy.start()
+    for copy in run_copies:
+        copy.wait_recv()
+    total = jnp.zeros((8, COLS), F32)
+    for k in range(GROUP):
+        chosen = (lane_t // THIN) % GROUP == behind[k]
+        moved = mark(chosen & (row_t == turn * PROBES + (lane_t // PROBES) * THIN + lane_t % THIN))
+        for piece in split3(run_in[k]):
+            total = total + dot(piece, moved)
+    grads_out[...] = total
     grads_in[me] = grads_out[...]
 
     def grads_copy(k):
@@ -582,13 +644,16 @@
         return carry
 
     lax.fori_loop(1, peers, finish, 0)
-    wait_departures(edge_copies)
-    wait_departures(cross_copies)
     for e in range(EXCHANGES):
         wait_departures(space_copies(e))
-        if e < ITERS:
-            for c in range(CHUNKS):
-                wait_departures(time_copies(e, c))
+        wait_departures(time_copies(e))
+    for copy in scales_copies + swap_copies + sums_copies + run_copies + back_copies:
+        copy.wait_send()
+    for copy in back_copies:
+        copy.wait_recv()
+    parted = [(kept, turn), (small, turn)] + [(back_in[k], behind[k]) for k in range(1, GROUP)]
+    for half, values in enumerate(put(parted, by_probe)):
+        sol_ref[half * HALF : (half + 1) * HALF, :] = values
     total = grads_in[0]
     for s in range(1, peers):
         total = total + grads_in[s]
@@ -644,25 +709,31 @@
             pltpu.VMEM((NODES_DEV, BLOCK), F32),
             pltpu.VMEM((NODES_DEV, WIDTH), BF16),
             pltpu.VMEM((EXCHANGES, WIDTH, COLS), BF16),
-            pltpu.VMEM((CHUNKS, BLOCK, BLOCK), BF16),
-            pltpu.VMEM((CHUNKS, BLOCK, BLOCK), BF16),
-            pltpu.VMEM((ITERS, CHUNKS, BLOCK, BLOCK), BF16),
-            pltpu.VMEM((ITERS, CHUNKS, BLOCK, BLOCK), BF16),
+            pltpu.VMEM((EXCHANGES, BLOCK, BLOCK), BF16),
+            pltpu.VMEM((EXCHANGES, BLOCK, BLOCK), BF16),
             pltpu.VMEM((EXCHANGES, HALO_ROWS, COLS), BF16),
             pltpu.VMEM((EXCHANGES, HALO_ROWS, COLS), BF16),
-            pltpu.VMEM((ITERS, CHUNKS, BLOCK, BLOCK), BF16),
-            pltpu.VMEM((ITERS, CHUNKS, BLOCK, BLOCK), BF16),
+            pltpu.VMEM((EXCHANGES, BLOCK, BLOCK), BF16),
+            pltpu.VMEM((EXCHANGES, BLOCK, BLOCK), BF16),
             pltpu.VMEM((NODES_DEV, COLS), F32),
+            pltpu.VMEM((NODES_DEV, COLS), BF16),
             pltpu.VMEM((NODES_DEV, COLS), F32),
-            pltpu.VMEM((8, BLOCK), F32),
-            pltpu.VMEM((2, 8, BLOCK), F32),
-            pltpu.VMEM((2, 8, BLOCK), F32),
-            pltpu.VMEM((2, 8, BLOCK), F32),
-            pltpu.VMEM((NODES_DEV, COLS), F32),
-            pltpu.VMEM((NODES_DEV, COLS), F32),
+            pltpu.VMEM((NODES_DEV, COLS), BF16),
+            pltpu.VMEM((GROUP, HALF, BLOCK), BF16),
+            pltpu.VMEM((GROUP, HALF, BLOCK), BF16),
+            pltpu.VMEM((GROUP, HALF, BLOCK), BF16),
+            pltpu.VMEM((GROUP, HALF, BLOCK), BF16),
+            pltpu.VMEM((8, COLS), F32),
+            pltpu.VMEM((GROUP, 8, COLS), F32),
+            pltpu.VMEM((CELLS, BLOCK), F32),
+            pltpu.VMEM((GROUP * CELLS, BLOCK), F32),
             pltpu.VMEM((8, COLS), jnp.int32),
             pltpu.VMEM((2, 8, COLS), jnp.int32),
             pltpu.VMEM((2, HALO_B, NB_DEV, 1, COLS), BF16),
+            pltpu.VMEM((NODES_DEV, COLS), F32),
+            pltpu.VMEM((NODES_DEV, COLS), F32),
+            pltpu.VMEM((8, COLS), F32),
+            pltpu.VMEM((GROUP, 8, COLS), F32),
             pltpu.VMEM((8, COLS), F32),
             pltpu.VMEM((peers, 8, COLS), F32),
             dma((12,)),
@@ -672,12 +743,18 @@
             dma((2,)),
             dma((EXCHANGES, 2)),
             dma((EXCHANGES, 2)),
-            dma((ITERS, CHUNKS, 2)),
-            dma((ITERS, CHUNKS, 2)),
-            dma((2,)),
-            dma((2,)),
-            dma((2,)),
-            dma((2,)),
+            dma((EXCHANGES, 2)),
+            dma((EXCHANGES, 2)),
+            dma((GROUP,)),
+            dma((GROUP,)),
+            dma((GROUP,)),
+            dma((GROUP,)),
+            dma((GROUP,)),
+            dma((GROUP,)),
+            dma((GROUP,)),
+            dma((GROUP,)),
+            dma((GROUP,)),
+            dma((GROUP,)),
             dma((peers,)),
             dma((peers,)),
         ],

time: 95.6 us -> 104 us (1.088); the launches traced: 95 us -> 102 us
  Pallas kernels: 91.5 us -> 98.8 us
    pallas_call x1, Pallas kernels: 91.5 us -> 98.8 us  [shards(): pl.pallas_call(functools.partial(kernel, peers, slabs, cap), out_shape=(j...]
where the time goes in v3:
time: 104 us; the launch traced here: 102 us
  Pallas kernels  98.8 us (95%)
  local copies, waits for them, and re-layouts  2.84 us (3%)
    pallas_call x1, Pallas kernels, shards(): pl.pallas_call(functools.partial(kernel, peers, slabs, cap), out_shape=(j...  98.8 us
    unnamed x4, local copies, waits for them, and re-layouts  2.84 us

profile of v3, /device:TPU:5, one launch (start us, length us, event | category | flops | bytes accessed | tf_op | source)
XLA Modules:
  0.0 102.3 jit_solution(7755701733936869942)
XLA Ops:
  0.6 98.8 %shard_map.131 = (f32[1024,256]{1,0:T(8,128)}, f32[2,256]{1,0:T(2,128)}) custom-call(bf16[1024,256]{1,0:T(8,128)(2,1)} %probe_hbm.1, f32[8,128]{1,0:T(8,128)} %bitcast.5, f32[4]{0:T(128)} %theta_space_hbm.1, f32[4]{0:T(128)} %theta_time_hbm.1, bf16[8,128,128]{2,1,0:T(8,128)(2,1)} %diag_hbm.1, bf16[8,8,128,128]{3,2,1,0:T(8,128)(2,1)} %off_hbm.1, ...), custom_call_target="tpu_custom_call" | custom-call | tf_op jit(solution)/shard_map/pallas_call | solution.py:682
  99.5 0.0 copy-start
  99.5 2.3 %copy.16 = f32[1024,256]{1,0:T(8,128)} copy(f32[1024,256]{1,0:T(8,128)} %get-tuple-element.4) | data formatting | bytes 2097152
  101.8 0.0 copy-done
  101.8 0.6 copy.17
Async XLA Ops:
  99.5 2.3 %copy-start = (f32[2,256]{1,0:T(2,128)S(1)}, f32[2,256]{1,0:T(2,128)}, u32[]{:S(2)}) copy-start(f32[2,256]{1,0:T(2,128)} %get-tuple-element.5) | copy-start | bytes 6148

commit v4 on v3

--- a/solution.py
+++ b/solution.py
@@ -140,6 +140,8 @@
     sums_recv_sem,
     run_send_sem,
     run_recv_sem,
+    coef_send_sem,
+    coef_recv_sem,
     grads_send_sem,
     grads_recv_sem,
 ):
@@ -151,6 +153,10 @@
     right = lax.rem(slab + GROUP, slabs)
     down = lax.rem(me + peers - 1, peers)
     up = lax.rem(me + 1, peers)
+    depth = lax.rem(me // 2, 2)
+    spot = (me // 4) * 2 + lax.rem(me, 2)
+    spots = peers // 2
+    partner = me + 2 - 4 * depth
     has_down, has_up = me > 0, me < peers - 1
     has_left, has_right = run > 0, run < slabs - GROUP
 
@@ -166,7 +172,7 @@
         (diag_hbm, diag),
         (off_hbm, off),
         (cols_hbm, cols),
-        (coef_hbm, coef),
+        (coef_hbm, coef.at[0]),
     )
     loads = [
         pltpu.make_async_copy(src, dst, load_sem.at[i]) for i, (src, dst) in enumerate(pairs)
@@ -185,8 +191,11 @@
     lax.fori_loop(1, peers, greet, 0)
     ahead = [run + lax.rem(turn + k, GROUP) for k in range(GROUP)]
     behind = [lax.rem(turn + GROUP - k, GROUP) for k in range(GROUP)]
+    across = run + lax.rem(turn + GROUP - 1 + 2 * depth, GROUP)
     for other in (left, right, *ahead[1:]):
         pl.semaphore_signal(barrier, inc=1, device_id=(me, other), device_id_type=MESH)
+    for other in ahead[1:]:
+        pl.semaphore_signal(barrier, inc=1, device_id=(partner, other), device_id_type=MESH)
 
     loads[0].wait()
     owner_cols = jnp.transpose(owner[...].astype(F32))
@@ -223,7 +232,28 @@
                 onehot[part, h : h + BLOCK] = mark(place == lanes + h)
         return dot(covt[...], onehot[...]).astype(BF16)
 
-    pl.semaphore_wait(barrier, peers + GROUP)
+    for i in (8, 9, 10):
+        loads[i].wait()
+
+    def combine(i, carry):
+        b = i // NB_DEV
+        rows = pl.ds(pl.multiple_of((i % NB_DEV) * 16, 16), 16)
+        parts = [off[b, k, rows, :].astype(F32) for k in range(NB_DEV)]
+        own = diag[b, rows, :].astype(F32)
+        columns = [cols[b, k] for k in range(NB_DEV)]
+        place = pl.ds(pl.multiple_of(i * 16, 16), 16)
+        for m in range(WIDTH // BLOCK):
+            total = jnp.zeros((16, BLOCK), F32)
+            for k in range(NB_DEV):
+                total = total + jnp.where(columns[k] == m, 1.0, 0.0) * parts[k]
+            if m < NB_DEV:
+                total = total + jnp.where(b == m, 1.0, 0.0) * own
+            comb[place, m * BLOCK : (m + 1) * BLOCK] = total.astype(BF16)
+        return carry
+
+    lax.fori_loop(0, NODES_DEV // 16, combine, 0)
+
+    pl.semaphore_wait(barrier, peers + 2 * GROUP - 1)
 
     loads[3].wait()
     sub8 = iota((8, COLS), 0)
@@ -246,7 +276,7 @@
     for copy in needs_copies:
         copy.start()
 
-    for i in range(4, 9):
+    for i in range(4, 8):
         loads[i].wait()
     col = iota((8, COLS), 1)
     sub8 = iota((8, COLS), 0)
@@ -278,8 +308,20 @@
     ]
     place = pl.ds(pl.multiple_of(turn * CELLS, CELLS), CELLS)
     sums_copies = [
-        group_copy(k, sums_out, sums_in.at[place], sums_send_sem, sums_recv_sem) for k in range(1, GROUP)
+        group_copy(k, sums_out.at[0], sums_in.at[0, place], sums_send_sem, sums_recv_sem)
+        for k in range(1, GROUP)
     ]
+    for k in range(GROUP):
+        sums_copies.append(
+            pltpu.make_async_remote_copy(
+                src_ref=sums_out.at[1],
+                dst_ref=sums_in.at[1, place],
+                send_sem=sums_send_sem.at[GROUP + k],
+                recv_sem=sums_recv_sem.at[GROUP + k],
+                device_id=(partner, ahead[k]),
+                device_id_type=MESH,
+            )
+        )
 
     tall, wide = (iota((COLS, BLOCK), i) for i in range(2))
     low_tall, high_wide = (iota((BLOCK, COLS), i) for i in range(2))
@@ -310,6 +352,23 @@
     for copy in scales_copies + swap_copies:
         copy.start()
 
+    loads[11].wait()
+    coef_copies = []
+    for i, target in enumerate((slab, across)):
+        rows = pl.ds(i * HALF, HALF)
+        coef_copies.append(
+            pltpu.make_async_remote_copy(
+                src_ref=coef.at[0, rows],
+                dst_ref=coef.at[1, rows],
+                send_sem=coef_send_sem.at[i],
+                recv_sem=coef_recv_sem.at[i],
+                device_id=(partner, target),
+                device_id_type=MESH,
+            )
+        )
+    for copy in coef_copies:
+        copy.start()
+
     def beside(sends, receives, src, dst, send_sem, recv_sem, target):
         copy = pltpu.make_async_remote_copy(
             src_ref=src,
@@ -353,14 +412,24 @@
             device_id_type=MESH,
         )
 
-    def send(k, carry):
-        target = lax.rem(me + k, peers)
-        send_obs[k] = compact(target)
-        obs_copy(k, target).start()
+    def place_of(i):
+        other = lax.rem(spot + i // 2, spots)
+        return (other // 2) * 4 + lax.rem(other, 2)
+
+    def owner_of(i):
+        return place_of(i) + 2 * lax.rem(depth + i, 2)
+
+    def target_of(i):
+        return place_of(i) + 2 * depth
+
+    def send(i, carry):
+        send_obs[i] = compact(owner_of(i))
+        obs_copy(i, target_of(i)).start()
         return carry
 
-    lax.fori_loop(1, peers, send, 0)
-    recv_obs[0] = compact(me)
+    lax.fori_loop(2, peers, send, 0)
+    for i in range(2):
+        recv_obs[i] = compact(owner_of(i))
 
     total = mine
     for k in range(1, GROUP):
@@ -460,27 +529,6 @@
     start_space(0)
     start_time(0)
 
-    loads[9].wait()
-    loads[10].wait()
-
-    def combine(i, carry):
-        b = i // NB_DEV
-        rows = pl.ds(pl.multiple_of((i % NB_DEV) * 16, 16), 16)
-        parts = [off[b, k, rows, :].astype(F32) for k in range(NB_DEV)]
-        own = diag[b, rows, :].astype(F32)
-        columns = [cols[b, k] for k in range(NB_DEV)]
-        place = pl.ds(pl.multiple_of(i * 16, 16), 16)
-        for m in range(WIDTH // BLOCK):
-            total = jnp.zeros((16, BLOCK), F32)
-            for k in range(NB_DEV):
-                total = total + jnp.where(columns[k] == m, 1.0, 0.0) * parts[k]
-            if m < NB_DEV:
-                total = total + jnp.where(b == m, 1.0, 0.0) * own
-            comb[place, m * BLOCK : (m + 1) * BLOCK] = total.astype(BF16)
-        return carry
-
-    lax.fori_loop(0, NODES_DEV // 16, combine, 0)
-
     row_t, lane_t = iota((COLS, COLS), 0), iota((COLS, COLS), 1)
     inner = jnp.where(
         row_t == lane_t, 2.0, jnp.where(jnp.abs(row_t - lane_t) == THIN, -1.0, 0.0)
@@ -521,11 +569,13 @@
 
     own_product(0)
 
-    loads[11].wait()
-    counted[...] = jnp.zeros((NODES_DEV, BLOCK), F32)
+    counted[...] = jnp.zeros_like(counted)
+    for copy in coef_copies:
+        copy.wait_recv()
     row_w = iota((BLOCK, cap), 0)
 
     def weigh(k):
+        which = lax.rem(k, 2)
         digits = recv_obs[k, NCOV:, :].astype(F32)
         live = digits[2:3, :] > 0.5
         number = (digits[0:1, :] * 64.0 + digits[1:2, :]).astype(jnp.int32)
@@ -535,7 +585,7 @@
         eta = jnp.zeros((1, cap), F32)
         for c in range(NODES_DEV // CHUNK):
             part = slice(c * CHUNK, (c + 1) * CHUNK)
-            scores = dot(coef[part, :], rows)
+            scores = dot(coef[which, part, :], rows)
             found = iota((CHUNK, cap), 0) + c * CHUNK == node
             eta = eta + jnp.sum(jnp.where(found, scores, 0.0), axis=0, keepdims=True)
             masks[part, :] = mark(found)
@@ -544,31 +594,33 @@
         spread = jnp.zeros((BLOCK, cap), F32)
         for i, piece in enumerate(pieces):
             spread = jnp.where(row_w == time + i * T_DEV, piece, spread)
-        counted[...] += lax.dot_general(
+        counted[which] += lax.dot_general(
             masks[...], spread.astype(BF16), NT_DIMS, preferred_element_type=F32
         )
 
     weigh(0)
+    weigh(1)
 
     def receive(k, carry):
-        obs_copy(k, lax.rem(me + k, peers)).wait_recv()
+        obs_copy(k, target_of(k)).wait_recv()
         weigh(k)
         return carry
 
-    lax.fori_loop(1, peers, receive, 0)
-
-    packed = jnp.zeros((BLOCK, BLOCK), F32)
-    for b in range(NB_DEV):
-        held = counted[b * BLOCK : (b + 1) * BLOCK, :]
-        held = held + pltpu.roll(held, BLOCK - T_DEV, 1) + pltpu.roll(held, BLOCK - 2 * T_DEV, 1)
-        packed = jnp.where(lanes // T_DEV == b, pltpu.roll(held, b * T_DEV, 1), packed)
-    sums_out[...] = jnp.transpose(packed)[:CELLS, :]
-    sums_in[place, :] = sums_out[...]
+    lax.fori_loop(2, peers, receive, 0)
+
+    for which in range(2):
+        packed = jnp.zeros((BLOCK, BLOCK), F32)
+        for b in range(NB_DEV):
+            held = counted[which, b * BLOCK : (b + 1) * BLOCK, :]
+            held = held + pltpu.roll(held, BLOCK - T_DEV, 1) + pltpu.roll(held, BLOCK - 2 * T_DEV, 1)
+            packed = jnp.where(lanes // T_DEV == b, pltpu.roll(held, b * T_DEV, 1), packed)
+        sums_out[which] = jnp.transpose(packed)[:CELLS, :]
     for copy in sums_copies:
         copy.start()
+    sums_in[0, place, :] = sums_out[0]
     for copy in sums_copies:
         copy.wait_recv()
-    pieces = split3(jnp.transpose(sums_in[...]))
+    pieces = split3(jnp.transpose(sums_in[0] + sums_in[1]))
     for b in range(NB_DEV):
         part = slice(b * BLOCK, (b + 1) * BLOCK)
         cell_of = (high_wide // PROBES) * CELLS + b * T_DEV + (high_wide // THIN) % T_DEV
@@ -640,14 +692,19 @@
 
     def finish(k, carry):
         grads_copy(k).wait()
-        obs_copy(k, lax.rem(me + k, peers)).wait_send()
         return carry
 
     lax.fori_loop(1, peers, finish, 0)
+
+    def sent(i, carry):
+        obs_copy(i, target_of(i)).wait_send()
+        return carry
+
+    lax.fori_loop(2, peers, sent, 0)
     for e in range(EXCHANGES):
         wait_departures(space_copies(e))
         wait_departures(time_copies(e))
-    for copy in scales_copies + swap_copies + sums_copies + run_copies + back_copies:
+    for copy in scales_copies + swap_copies + coef_copies + sums_copies + run_copies + back_copies:
         copy.wait_send()
     for copy in back_copies:
         copy.wait_recv()
@@ -699,14 +756,14 @@
             pltpu.VMEM((OBS_DEV, NCOV), BF16),
             pltpu.VMEM((OBS_DEV // BLOCK, BLOCK), jnp.int32),
             pltpu.VMEM((OBS_DEV // BLOCK, BLOCK), jnp.int32),
-            pltpu.VMEM((NODES_DEV, NCOV), BF16),
+            pltpu.VMEM((2, NODES_DEV, NCOV), BF16),
             pltpu.VMEM((OBS_DEV, BLOCK), jnp.int32),
             pltpu.VMEM((ROWS, OBS_DEV), BF16),
             pltpu.VMEM((OBS_DEV, cap), BF16),
             pltpu.VMEM((peers, ROWS, cap), BF16),
             pltpu.VMEM((peers, ROWS, cap), BF16),
             pltpu.VMEM((NODES_DEV, cap), BF16),
-            pltpu.VMEM((NODES_DEV, BLOCK), F32),
+            pltpu.VMEM((2, NODES_DEV, BLOCK), F32),
             pltpu.VMEM((NODES_DEV, WIDTH), BF16),
             pltpu.VMEM((EXCHANGES, WIDTH, COLS), BF16),
             pltpu.VMEM((EXCHANGES, BLOCK, BLOCK), BF16),
@@ -725,8 +782,8 @@
             pltpu.VMEM((GROUP, HALF, BLOCK), BF16),
             pltpu.VMEM((8, COLS), F32),
             pltpu.VMEM((GROUP, 8, COLS), F32),
-            pltpu.VMEM((CELLS, BLOCK), F32),
-            pltpu.VMEM((GROUP * CELLS, BLOCK), F32),
+            pltpu.VMEM((2, CELLS, BLOCK), F32),
+            pltpu.VMEM((2, GROUP * CELLS, BLOCK), F32),
             pltpu.VMEM((8, COLS), jnp.int32),
             pltpu.VMEM((2, 8, COLS), jnp.int32),
             pltpu.VMEM((2, HALO_B, NB_DEV, 1, COLS), BF16),
@@ -751,10 +808,12 @@
             dma((GROUP,)),
             dma((GROUP,)),
             dma((GROUP,)),
+            dma((2 * GROUP,)),
+            dma((2 * GROUP,)),
             dma((GROUP,)),
             dma((GROUP,)),
-            dma((GROUP,)),
-            dma((GROUP,)),
+            dma((2,)),
+            dma((2,)),
             dma((peers,)),
             dma((peers,)),
         ],

time: 104 us -> 105 us (level); the launches traced: 102 us -> 104 us
  Pallas kernels: 98.8 us -> 101 us
    pallas_call x1, Pallas kernels: 98.8 us -> 101 us  [shards(): pl.pallas_call(functools.partial(kernel, peers, slabs, cap), out_shape=(j...]
where the time goes in v4:
time: 105 us; the launch traced here: 104 us
  Pallas kernels  101 us (96%)
  local copies, waits for them, and re-layouts  2.84 us (3%)
    pallas_call x1, Pallas kernels, shards(): pl.pallas_call(functools.partial(kernel, peers, slabs, cap), out_shape=(j...  101 us
    unnamed x4, local copies, waits for them, and re-layouts  2.84 us

profile of v4, /device:TPU:5, one launch (start us, length us, event | category | flops | bytes accessed | tf_op | source)
XLA Modules:
  0.0 104.4 jit_solution(822222932471698378)
XLA Ops:
  0.6 100.9 %shard_map.131 = (f32[1024,256]{1,0:T(8,128)}, f32[2,256]{1,0:T(2,128)}) custom-call(bf16[1024,256]{1,0:T(8,128)(2,1)} %probe_hbm.1, f32[8,128]{1,0:T(8,128)} %bitcast.5, f32[4]{0:T(128)} %theta_space_hbm.1, f32[4]{0:T(128)} %theta_time_hbm.1, bf16[8,128,128]{2,1,0:T(8,128)(2,1)} %diag_hbm.1, bf16[8,8,128,128]{3,2,1,0:T(8,128)(2,1)} %off_hbm.1, ...), custom_call_target="tpu_custom_call" | custom-call | tf_op jit(solution)/shard_map/pallas_call | solution.py:739
  101.6 0.0 copy-start
  101.6 2.3 %copy.16 = f32[1024,256]{1,0:T(8,128)} copy(f32[1024,256]{1,0:T(8,128)} %get-tuple-element.4) | data formatting | bytes 2097152
  103.8 0.0 copy-done
  103.8 0.6 copy.17
Async XLA Ops:
  101.6 2.3 %copy-start = (f32[2,256]{1,0:T(2,128)S(1)}, f32[2,256]{1,0:T(2,128)}, u32[]{:S(2)}) copy-start(f32[2,256]{1,0:T(2,128)} %get-tuple-element.5) | copy-start | bytes 6148

commit v5 on v2

--- a/solution.py
+++ b/solution.py
@@ -23,6 +23,9 @@
 EXCHANGES = ITERS + 1
 CHUNK = 256
 CHUNKS = NODES_DEV // CHUNK
+GROUP = 4
+HALF = NODES_DEV // 2
+CELLS = NB_DEV * T_DEV
 
 RELAX = 0.6
 MESH = pl.DeviceIdType.MESH
@@ -109,6 +112,8 @@
     needs_out,
     needs_in,
     picks,
+    sums_out,
+    sums_in,
     grads_out,
     grads_in,
     load_sem,
@@ -126,6 +131,10 @@
     cross_recv_sem,
     grads_send_sem,
     grads_recv_sem,
+    coef_send_sem,
+    coef_recv_sem,
+    sums_send_sem,
+    sums_recv_sem,
 ):
     me = lax.axis_index("space")
     slab = lax.axis_index("tm")
@@ -133,6 +142,12 @@
     right = lax.rem(slab + 1, slabs)
     down = lax.rem(me + peers - 1, peers)
     up = lax.rem(me + 1, peers)
+    depth = lax.rem(me // 2, 2)
+    spot = (me // 4) * 2 + lax.rem(me, 2)
+    spots = peers // 2
+    partner = me + 2 - 4 * depth
+    turn = lax.rem(slab, GROUP)
+    across = slab - turn + lax.rem(turn + GROUP - 1 + 2 * depth, GROUP)
     has_down, has_up = me > 0, me < peers - 1
     has_left, has_right = slab > 0, slab < slabs - 1
 
@@ -148,7 +163,7 @@
         (diag_hbm, diag),
         (off_hbm, off),
         (cols_hbm, cols),
-        (coef_hbm, coef),
+        (coef_hbm, coef.at[0]),
     )
     loads = [
         pltpu.make_async_copy(src, dst, load_sem.at[i]) for i, (src, dst) in enumerate(pairs)
@@ -165,8 +180,8 @@
         return carry
 
     lax.fori_loop(1, peers, greet, 0)
-    for other in (left, right):
-        pl.semaphore_signal(barrier, inc=1, device_id=(me, other), device_id_type=MESH)
+    for target in ((me, left), (me, right), (partner, across)):
+        pl.semaphore_signal(barrier, inc=1, device_id=target, device_id_type=MESH)
 
     loads[0].wait()
     owner_cols = jnp.transpose(owner[...].astype(F32))
@@ -203,7 +218,28 @@
                 onehot[part, h : h + BLOCK] = mark(place == lanes + h)
         return dot(covt[...], onehot[...]).astype(BF16)
 
-    pl.semaphore_wait(barrier, peers + 1)
+    for i in (8, 9, 10):
+        loads[i].wait()
+
+    def combine(i, carry):
+        b = i // NB_DEV
+        rows = pl.ds(pl.multiple_of((i % NB_DEV) * 16, 16), 16)
+        parts = [off[b, k, rows, :].astype(F32) for k in range(NB_DEV)]
+        own = diag[b, rows, :].astype(F32)
+        columns = [cols[b, k] for k in range(NB_DEV)]
+        place = pl.ds(pl.multiple_of(i * 16, 16), 16)
+        for m in range(WIDTH // BLOCK):
+            total = jnp.zeros((16, BLOCK), F32)
+            for k in range(NB_DEV):
+                total = total + jnp.where(columns[k] == m, 1.0, 0.0) * parts[k]
+            if m < NB_DEV:
+                total = total + jnp.where(b == m, 1.0, 0.0) * own
+            comb[place, m * BLOCK : (m + 1) * BLOCK] = total.astype(BF16)
+        return carry
+
+    lax.fori_loop(0, NODES_DEV // 16, combine, 0)
+
+    pl.semaphore_wait(barrier, peers + 2)
 
     loads[3].wait()
     sub8 = iota((8, COLS), 0)
@@ -226,7 +262,7 @@
     for copy in needs_copies:
         copy.start()
 
-    for i in range(4, 9):
+    for i in range(4, 8):
         loads[i].wait()
     sub_e = iota((8, BLOCK), 0)
     ends = (theta_space[T_DEV - 1], theta_time[T_DEV - 1], theta_space[0], theta_time[0])
@@ -273,6 +309,32 @@
 
     start_copies(edge_copies)
 
+    loads[11].wait()
+    coef_copies = []
+    for i, target in enumerate((slab, across)):
+        rows = pl.ds(i * HALF, HALF)
+        coef_copies.append(
+            pltpu.make_async_remote_copy(
+                src_ref=coef.at[0, rows],
+                dst_ref=coef.at[1, rows],
+                send_sem=coef_send_sem.at[i],
+                recv_sem=coef_recv_sem.at[i],
+                device_id=(partner, target),
+                device_id_type=MESH,
+            )
+        )
+    for copy in coef_copies:
+        copy.start()
+    sums_copy = pltpu.make_async_remote_copy(
+        src_ref=sums_out,
+        dst_ref=sums_in.at[pl.ds(0, CELLS)],
+        send_sem=sums_send_sem,
+        recv_sem=sums_recv_sem,
+        device_id=(partner, slab),
+        device_id_type=MESH,
+    )
+    sums_in[CELLS:, :] = jnp.zeros((BLOCK - CELLS, BLOCK), F32)
+
     def obs_copy(k, target):
         return pltpu.make_async_remote_copy(
             src_ref=send_obs.at[k],
@@ -283,14 +345,24 @@
             device_id_type=MESH,
         )
 
-    def send(k, carry):
-        target = lax.rem(me + k, peers)
-        send_obs[k] = compact(target)
-        obs_copy(k, target).start()
+    def place_of(i):
+        other = lax.rem(spot + i // 2, spots)
+        return (other // 2) * 4 + lax.rem(other, 2)
+
+    def owner_of(i):
+        return place_of(i) + 2 * lax.rem(depth + i, 2)
+
+    def target_of(i):
+        return place_of(i) + 2 * depth
+
+    def send(i, carry):
+        send_obs[i] = compact(owner_of(i))
+        obs_copy(i, target_of(i)).start()
         return carry
 
-    lax.fori_loop(1, peers, send, 0)
-    recv_obs[0] = compact(me)
+    lax.fori_loop(2, peers, send, 0)
+    for i in range(2):
+        recv_obs[i] = compact(owner_of(i))
 
     col_time = iota((1, COLS), 1) // PROBES
     scale_space = jnp.zeros((1, COLS), F32)
@@ -398,27 +470,6 @@
     for c in range(CHUNKS):
         start_time(0, c, probe[c * CHUNK : (c + 1) * CHUNK, :].astype(F32))
 
-    loads[9].wait()
-    loads[10].wait()
-
-    def combine(i, carry):
-        b = i // NB_DEV
-        rows = pl.ds(pl.multiple_of((i % NB_DEV) * 16, 16), 16)
-        parts = [off[b, k, rows, :].astype(F32) for k in range(NB_DEV)]
-        own = diag[b, rows, :].astype(F32)
-        columns = [cols[b, k] for k in range(NB_DEV)]
-        place = pl.ds(pl.multiple_of(i * 16, 16), 16)
-        for m in range(WIDTH // BLOCK):
-            total = jnp.zeros((16, BLOCK), F32)
-            for k in range(NB_DEV):
-                total = total + jnp.where(columns[k] == m, 1.0, 0.0) * parts[k]
-            if m < NB_DEV:
-                total = total + jnp.where(b == m, 1.0, 0.0) * own
-            comb[place, m * BLOCK : (m + 1) * BLOCK] = total.astype(BF16)
-        return carry
-
-    lax.fori_loop(0, NODES_DEV // 16, combine, 0)
-
     row_t, lane_t = iota((COLS, COLS), 0), iota((COLS, COLS), 1)
     inner = jnp.where(
         row_t == lane_t, 2.0, jnp.where(jnp.abs(row_t - lane_t) == PROBES, -1.0, 0.0)
@@ -460,11 +511,13 @@
 
     own_product(0)
 
-    loads[11].wait()
-    counted[...] = jnp.zeros((NODES_DEV, BLOCK), F32)
+    counted[...] = jnp.zeros_like(counted)
+    for copy in coef_copies:
+        copy.wait_recv()
     row_w = iota((BLOCK, cap), 0)
 
     def weigh(k):
+        which = lax.rem(k, 2)
         digits = recv_obs[k, NCOV:, :].astype(F32)
         live = digits[2:3, :] > 0.5
         number = (digits[0:1, :] * 64.0 + digits[1:2, :]).astype(jnp.int32)
@@ -474,7 +527,7 @@
         eta = jnp.zeros((1, cap), F32)
         for c in range(NODES_DEV // CHUNK):
             part = slice(c * CHUNK, (c + 1) * CHUNK)
-            scores = dot(coef[part, :], rows)
+            scores = dot(coef[which, part, :], rows)
             found = iota((CHUNK, cap), 0) + c * CHUNK == node
             eta = eta + jnp.sum(jnp.where(found, scores, 0.0), axis=0, keepdims=True)
             masks[part, :] = mark(found)
@@ -483,26 +536,31 @@
         spread = jnp.zeros((BLOCK, cap), F32)
         for i, piece in enumerate(pieces):
             spread = jnp.where(row_w == time + i * T_DEV, piece, spread)
-        counted[...] += lax.dot_general(
+        counted[which] += lax.dot_general(
             masks[...], spread.astype(BF16), NT_DIMS, preferred_element_type=F32
         )
 
     weigh(0)
+    weigh(1)
 
     def receive(k, carry):
-        obs_copy(k, lax.rem(me + k, peers)).wait_recv()
+        obs_copy(k, target_of(k)).wait_recv()
         weigh(k)
         return carry
 
-    lax.fori_loop(1, peers, receive, 0)
-
-    spread_row, spread_col = iota((BLOCK, COLS), 0), iota((BLOCK, COLS), 1) // PROBES
-    repeat = mark((spread_row < 3 * T_DEV) & (spread_row % T_DEV == spread_col))
-    for _, part in parts():
-        pieces = split3(counted[part, :])
-        obs_diag = dot(pieces[0], repeat) + dot(pieces[1], repeat) + dot(pieces[2], repeat)
-        local_diag[part, :] = local_diag[part, :] + obs_diag
-        step[part, :] = RELAX / (step[part, :] + obs_diag)
+    lax.fori_loop(2, peers, receive, 0)
+
+    def pack_sums(which):
+        packed = jnp.zeros((BLOCK, BLOCK), F32)
+        for b in range(NB_DEV):
+            held = counted[which, b * BLOCK : (b + 1) * BLOCK, :]
+            held = held + pltpu.roll(held, BLOCK - T_DEV, 1) + pltpu.roll(held, BLOCK - 2 * T_DEV, 1)
+            packed = jnp.where(lanes // T_DEV == b, pltpu.roll(held, b * T_DEV, 1), packed)
+        return packed
+
+    sums_out[...] = jnp.transpose(pack_sums(1))[:CELLS, :]
+    sums_copy.start()
+    own_sums = pack_sums(0)
 
     wait_arrivals(edge_copies)
     for c in range(CHUNKS):
@@ -513,6 +571,16 @@
         for side, row, first, later in ((0, 0, first_low, time_low), (1, 2, first_high, time_high)):
             base = edges_in[side, row : row + 1, :] * sdiag + 2.0 * edges_in[side, row + 1 : row + 2, :] + nugget
             later[0, c] = (RELAX * first[c].astype(F32) / base).astype(BF16)
+
+    sums_copy.wait_recv()
+    pieces = split3(own_sums + jnp.transpose(sums_in[...]))
+    cell_row, cell_col = iota((BLOCK, COLS), 0), iota((BLOCK, COLS), 1) // PROBES
+    for b in range(NB_DEV):
+        part = slice(b * BLOCK, (b + 1) * BLOCK)
+        repeat = mark(cell_row == b * T_DEV + cell_col)
+        obs_diag = dot(pieces[0], repeat) + dot(pieces[1], repeat) + dot(pieces[2], repeat)
+        local_diag[part, :] = local_diag[part, :] + obs_diag
+        step[part, :] = RELAX / (step[part, :] + obs_diag)
 
     crossed = [jnp.zeros((1, BLOCK), F32), jnp.zeros((1, BLOCK), F32)]
     for e in range(ITERS):
@@ -578,10 +646,18 @@
 
     def finish(k, carry):
         grads_copy(k).wait()
-        obs_copy(k, lax.rem(me + k, peers)).wait_send()
         return carry
 
     lax.fori_loop(1, peers, finish, 0)
+
+    def sent(i, carry):
+        obs_copy(i, target_of(i)).wait_send()
+        return carry
+
+    lax.fori_loop(2, peers, sent, 0)
+    sums_copy.wait_send()
+    for copy in coef_copies:
+        copy.wait_send()
     wait_departures(edge_copies)
     wait_departures(cross_copies)
     for e in range(EXCHANGES):
@@ -634,14 +710,14 @@
             pltpu.VMEM((OBS_DEV, NCOV), BF16),
             pltpu.VMEM((OBS_DEV // BLOCK, BLOCK), jnp.int32),
             pltpu.VMEM((OBS_DEV // BLOCK, BLOCK), jnp.int32),
-            pltpu.VMEM((NODES_DEV, NCOV), BF16),
+            pltpu.VMEM((2, NODES_DEV, NCOV), BF16),
             pltpu.VMEM((OBS_DEV, BLOCK), jnp.int32),
             pltpu.VMEM((ROWS, OBS_DEV), BF16),
             pltpu.VMEM((OBS_DEV, cap), BF16),
             pltpu.VMEM((peers, ROWS, cap), BF16),
             pltpu.VMEM((peers, ROWS, cap), BF16),
             pltpu.VMEM((NODES_DEV, cap), BF16),
-            pltpu.VMEM((NODES_DEV, BLOCK), F32),
+            pltpu.VMEM((2, NODES_DEV, BLOCK), F32),
             pltpu.VMEM((NODES_DEV, WIDTH), BF16),
             pltpu.VMEM((EXCHANGES, WIDTH, COLS), BF16),
             pltpu.VMEM((CHUNKS, BLOCK, BLOCK), BF16),
@@ -663,6 +739,8 @@
             pltpu.VMEM((8, COLS), jnp.int32),
             pltpu.VMEM((2, 8, COLS), jnp.int32),
             pltpu.VMEM((2, HALO_B, NB_DEV, 1, COLS), BF16),
+            pltpu.VMEM((CELLS, BLOCK), F32),
+            pltpu.VMEM((BLOCK, BLOCK), F32),
             pltpu.VMEM((8, COLS), F32),
             pltpu.VMEM((peers, 8, COLS), F32),
             dma((12,)),
@@ -680,6 +758,10 @@
             dma((2,)),
             dma((peers,)),
             dma((peers,)),
+            dma((2,)),
+            dma((2,)),
+            dma,
+            dma,
         ],
         compiler_params=pltpu.CompilerParams(
             collective_id=0,

time: 95.6 us -> 97.7 us (1.022)
  Pallas kernels: 91.5 us -> 94 us
    pallas_call x1, Pallas kernels: 91.5 us -> 94 us  [shards(): pl.pallas_call(functools.partial(kernel, peers, slabs, cap), out_shape=(j...]
where the time goes in v5:
time: 97.7 us; the launch traced here: 97.5 us
  Pallas kernels  94 us (96%)
  local copies, waits for them, and re-layouts  2.84 us (3%)
    pallas_call x1, Pallas kernels, shards(): pl.pallas_call(functools.partial(kernel, peers, slabs, cap), out_shape=(j...  94 us
    unnamed x4, local copies, waits for them, and re-layouts  2.84 us

profile of v5, /device:TPU:5, one launch (start us, length us, event | category | flops | bytes accessed | tf_op | source)
XLA Modules:
  0.0 97.5 jit_solution(6116367524109759954)
XLA Ops:
  0.6 94.0 %shard_map.131 = (f32[1024,256]{1,0:T(8,128)}, f32[2,256]{1,0:T(2,128)}) custom-call(bf16[1024,256]{1,0:T(8,128)(2,1)} %probe_hbm.1, f32[8,128]{1,0:T(8,128)} %bitcast.5, f32[4]{0:T(128)} %theta_space_hbm.1, f32[4]{0:T(128)} %theta_time_hbm.1, bf16[8,128,128]{2,1,0:T(8,128)(2,1)} %diag_hbm.1, bf16[8,8,128,128]{3,2,1,0:T(8,128)(2,1)} %off_hbm.1, ...), custom_call_target="tpu_custom_call" | custom-call | tf_op jit(solution)/shard_map/pallas_call | solution.py:693
  94.7 0.0 copy-start
  94.7 2.3 %copy.16 = f32[1024,256]{1,0:T(8,128)} copy(f32[1024,256]{1,0:T(8,128)} %get-tuple-element.4) | data formatting | bytes 2097152
  97.0 0.0 copy-done
  97.0 0.6 copy.17
Async XLA Ops:
  94.7 2.3 %copy-start = (f32[2,256]{1,0:T(2,128)S(1)}, f32[2,256]{1,0:T(2,128)}, u32[]{:S(2)}) copy-start(f32[2,256]{1,0:T(2,128)} %get-tuple-element.5) | copy-start | bytes 6148

commit v6 on v2

--- a/solution.py
+++ b/solution.py
@@ -203,6 +203,27 @@
                 onehot[part, h : h + BLOCK] = mark(place == lanes + h)
         return dot(covt[...], onehot[...]).astype(BF16)
 
+    for i in (8, 9, 10):
+        loads[i].wait()
+
+    def combine(i, carry):
+        b = i // NB_DEV
+        rows = pl.ds(pl.multiple_of((i % NB_DEV) * 16, 16), 16)
+        parts = [off[b, k, rows, :].astype(F32) for k in range(NB_DEV)]
+        own = diag[b, rows, :].astype(F32)
+        columns = [cols[b, k] for k in range(NB_DEV)]
+        place = pl.ds(pl.multiple_of(i * 16, 16), 16)
+        for m in range(WIDTH // BLOCK):
+            total = jnp.zeros((16, BLOCK), F32)
+            for k in range(NB_DEV):
+                total = total + jnp.where(columns[k] == m, 1.0, 0.0) * parts[k]
+            if m < NB_DEV:
+                total = total + jnp.where(b == m, 1.0, 0.0) * own
+            comb[place, m * BLOCK : (m + 1) * BLOCK] = total.astype(BF16)
+        return carry
+
+    lax.fori_loop(0, NODES_DEV // 16, combine, 0)
+
     pl.semaphore_wait(barrier, peers + 1)
 
     loads[3].wait()
@@ -226,7 +247,7 @@
     for copy in needs_copies:
         copy.start()
 
-    for i in range(4, 9):
+    for i in range(4, 8):
         loads[i].wait()
     sub_e = iota((8, BLOCK), 0)
     ends = (theta_space[T_DEV - 1], theta_time[T_DEV - 1], theta_space[0], theta_time[0])
@@ -283,13 +304,20 @@
             device_id_type=MESH,
         )
 
+    far = peers // 4
+
+    def in_turn(j):
+        kind = lax.rem(j, 3)
+        return far * (2 - kind + 3 * (kind // 2)) + j // 3
+
     def send(k, carry):
         target = lax.rem(me + k, peers)
         send_obs[k] = compact(target)
         obs_copy(k, target).start()
         return carry
 
-    lax.fori_loop(1, peers, send, 0)
+    lax.fori_loop(0, 3 * far, lambda j, carry: send(in_turn(j), carry), 0)
+    lax.fori_loop(1, far, send, 0)
     recv_obs[0] = compact(me)
 
     col_time = iota((1, COLS), 1) // PROBES
@@ -309,9 +337,9 @@
         base = scale_space * sdiag + 2.0 * scale_time + kappa_col
         step[part, :] = base
         local_diag[part, :] = jnp.broadcast_to(kappa_col, (BLOCK, COLS))
-        start = RELAX * probe[part, :].astype(F32) / base
+        start = probe[part, :].astype(F32) / base
         sol_ref[part, :] = start
-        field[0, part, :] = start.astype(BF16)
+        field[0, part, :] = (RELAX * start).astype(BF16)
 
     for e in range(EXCHANGES):
 
@@ -398,27 +426,6 @@
     for c in range(CHUNKS):
         start_time(0, c, probe[c * CHUNK : (c + 1) * CHUNK, :].astype(F32))
 
-    loads[9].wait()
-    loads[10].wait()
-
-    def combine(i, carry):
-        b = i // NB_DEV
-        rows = pl.ds(pl.multiple_of((i % NB_DEV) * 16, 16), 16)
-        parts = [off[b, k, rows, :].astype(F32) for k in range(NB_DEV)]
-        own = diag[b, rows, :].astype(F32)
-        columns = [cols[b, k] for k in range(NB_DEV)]
-        place = pl.ds(pl.multiple_of(i * 16, 16), 16)
-        for m in range(WIDTH // BLOCK):
-            total = jnp.zeros((16, BLOCK), F32)
-            for k in range(NB_DEV):
-                total = total + jnp.where(columns[k] == m, 1.0, 0.0) * parts[k]
-            if m < NB_DEV:
-                total = total + jnp.where(b == m, 1.0, 0.0) * own
-            comb[place, m * BLOCK : (m + 1) * BLOCK] = total.astype(BF16)
-        return carry
-
-    lax.fori_loop(0, NODES_DEV // 16, combine, 0)
-
     row_t, lane_t = iota((COLS, COLS), 0), iota((COLS, COLS), 1)
     inner = jnp.where(
         row_t == lane_t, 2.0, jnp.where(jnp.abs(row_t - lane_t) == PROBES, -1.0, 0.0)
@@ -453,8 +460,9 @@
             [jnp.where(lower_half, 0.0, pltpu.roll(high, PROBES, 1)), jnp.where(lower_half, 0.0, high)], axis=0
         )
         left_over = residual[part, :] + jnp.concatenate([first, last], axis=1)
-        solved = sol_ref[part, :] + step[part, :] * left_over
-        sol_ref[part, :] = solved
+        scaled = sol_ref[part, :] + step[part, :] * left_over
+        sol_ref[part, :] = scaled
+        solved = RELAX * scaled
         field[e + 1, part, :] = solved.astype(BF16)
         return solved
 
@@ -494,7 +502,8 @@
         weigh(k)
         return carry
 
-    lax.fori_loop(1, peers, receive, 0)
+    lax.fori_loop(0, 3 * far, lambda j, carry: receive(in_turn(j), carry), 0)
+    lax.fori_loop(1, far, receive, 0)
 
     spread_row, spread_col = iota((BLOCK, COLS), 0), iota((BLOCK, COLS), 1) // PROBES
     repeat = mark((spread_row < 3 * T_DEV) & (spread_row % T_DEV == spread_col))
@@ -502,7 +511,7 @@
         pieces = split3(counted[part, :])
         obs_diag = dot(pieces[0], repeat) + dot(pieces[1], repeat) + dot(pieces[2], repeat)
         local_diag[part, :] = local_diag[part, :] + obs_diag
-        step[part, :] = RELAX / (step[part, :] + obs_diag)
+        step[part, :] = 1.0 / (step[part, :] + obs_diag)
 
     wait_arrivals(edge_copies)
     for c in range(CHUNKS):
@@ -512,7 +521,7 @@
         nugget = jnp.where(lower_half, kappa_cols[:, lo : lo + 1], kappa_cols[:, hi : hi + 1])
         for side, row, first, later in ((0, 0, first_low, time_low), (1, 2, first_high, time_high)):
             base = edges_in[side, row : row + 1, :] * sdiag + 2.0 * edges_in[side, row + 1 : row + 2, :] + nugget
-            later[0, c] = (RELAX * first[c].astype(F32) / base).astype(BF16)
+            later[0, c] = (RELAX * (first[c].astype(F32) / base)).astype(BF16)
 
     crossed = [jnp.zeros((1, BLOCK), F32), jnp.zeros((1, BLOCK), F32)]
     for e in range(ITERS):
@@ -592,7 +601,7 @@
     total = grads_in[0]
     for s in range(1, peers):
         total = total + grads_in[s]
-    grads_ref[...] = total[0:2, :] / (NODES_DEV * peers)
+    grads_ref[...] = total[0:2, :]
 
 
 def shards(
@@ -614,7 +623,7 @@
     cap = 2 * OBS_DEV // peers
     vmem = pl.BlockSpec(memory_space=pltpu.VMEM)
     dma = pltpu.SemaphoreType.DMA
-    return pl.pallas_call(
+    scaled, totals = pl.pallas_call(
         functools.partial(kernel, peers, slabs, cap),
         out_shape=(
             jax.ShapeDtypeStruct((NODES_DEV, COLS), F32),
@@ -700,6 +709,7 @@
         obs_cell.reshape(OBS_DEV // BLOCK, BLOCK),
         svc_coef,
     )
+    return RELAX * scaled, totals / (NODES_DEV * peers)
 
 
 def solution(mesh):

time: 95.6 us -> 104 us (1.088)
  the two profiles are of different devices: /device:TPU:5 before, /device:TPU:69 now
where the time goes in v6:
time: 104 us
  Pallas kernels  100 us (96%)
  other arithmetic  2.87 us (3%)
    pallas_call x1, Pallas kernels, shards(): pl.pallas_call(functools.partial(kernel, peers, slabs, cap), out_shape=(j...  100 us
    mul x1, other arithmetic, shards(): return (RELAX * scaled, totals / (NODES_DEV * peers))  2.29 us

profile of v6, /device:TPU:69, one launch (start us, length us, event | category | flops | bytes accessed | tf_op | source)
XLA Modules:
  0.0 103.5 jit_solution(12673686587184521318)
XLA Ops:
  0.6 100.0 %shard_map.131 = (f32[1024,256]{1,0:T(8,128)}, f32[2,256]{1,0:T(2,128)}) custom-call(bf16[1024,256]{1,0:T(8,128)(2,1)} %probe_hbm.1, f32[8,128]{1,0:T(8,128)} %bitcast.5, f32[4]{0:T(128)} %theta_space_hbm.1, f32[4]{0:T(128)} %theta_time_hbm.1, bf16[8,128,128]{2,1,0:T(8,128)(2,1)} %diag_hbm.1, bf16[8,8,128,128]{3,2,1,0:T(8,128)(2,1)} %off_hbm.1, ...), custom_call_target="tpu_custom_call" | custom-call | tf_op jit(solution)/shard_map/pallas_call | solution.py:626
  100.6 0.0 copy-start
  100.7 2.3 %broadcast_multiply_fusion = f32[1024,256]{1,0:T(8,128)} fusion(f32[1024,256]{1,0:T(8,128)} %get-tuple-element.4), kind=kLoop, calls=%fused_computation | loop fusion | flops 262144 | bytes 2097152 | tf_op jit(solution)/shard_map/mul | solution.py:712
  102.9 0.0 copy-done
  102.9 0.6 broadcast_multiply_fusion.1
Async XLA Ops:
  100.6 2.3 %copy-start = (f32[2,256]{1,0:T(2,128)S(1)}, f32[2,256]{1,0:T(2,128)}, u32[]{:S(2)}) copy-start(f32[2,256]{1,0:T(2,128)} %get-tuple-element.5) | copy-start | bytes 6148

commit v7 on v5

--- a/solution.py
+++ b/solution.py
@@ -218,27 +218,6 @@
                 onehot[part, h : h + BLOCK] = mark(place == lanes + h)
         return dot(covt[...], onehot[...]).astype(BF16)
 
-    for i in (8, 9, 10):
-        loads[i].wait()
-
-    def combine(i, carry):
-        b = i // NB_DEV
-        rows = pl.ds(pl.multiple_of((i % NB_DEV) * 16, 16), 16)
-        parts = [off[b, k, rows, :].astype(F32) for k in range(NB_DEV)]
-        own = diag[b, rows, :].astype(F32)
-        columns = [cols[b, k] for k in range(NB_DEV)]
-        place = pl.ds(pl.multiple_of(i * 16, 16), 16)
-        for m in range(WIDTH // BLOCK):
-            total = jnp.zeros((16, BLOCK), F32)
-            for k in range(NB_DEV):
-                total = total + jnp.where(columns[k] == m, 1.0, 0.0) * parts[k]
-            if m < NB_DEV:
-                total = total + jnp.where(b == m, 1.0, 0.0) * own
-            comb[place, m * BLOCK : (m + 1) * BLOCK] = total.astype(BF16)
-        return carry
-
-    lax.fori_loop(0, NODES_DEV // 16, combine, 0)
-
     pl.semaphore_wait(barrier, peers + 2)
 
     loads[3].wait()
@@ -262,7 +241,7 @@
     for copy in needs_copies:
         copy.start()
 
-    for i in range(4, 8):
+    for i in range(4, 9):
         loads[i].wait()
     sub_e = iota((8, BLOCK), 0)
     ends = (theta_space[T_DEV - 1], theta_time[T_DEV - 1], theta_space[0], theta_time[0])
@@ -469,6 +448,27 @@
     start_space(0)
     for c in range(CHUNKS):
         start_time(0, c, probe[c * CHUNK : (c + 1) * CHUNK, :].astype(F32))
+
+    for i in (9, 10):
+        loads[i].wait()
+
+    def combine(i, carry):
+        b = i // NB_DEV
+        rows = pl.ds(pl.multiple_of((i % NB_DEV) * 16, 16), 16)
+        parts = [off[b, k, rows, :].astype(F32) for k in range(NB_DEV)]
+        own = diag[b, rows, :].astype(F32)
+        columns = [cols[b, k] for k in range(NB_DEV)]
+        place = pl.ds(pl.multiple_of(i * 16, 16), 16)
+        for m in range(WIDTH // BLOCK):
+            total = jnp.zeros((16, BLOCK), F32)
+            for k in range(NB_DEV):
+                total = total + jnp.where(columns[k] == m, 1.0, 0.0) * parts[k]
+            if m < NB_DEV:
+                total = total + jnp.where(b == m, 1.0, 0.0) * own
+            comb[place, m * BLOCK : (m + 1) * BLOCK] = total.astype(BF16)
+        return carry
+
+    lax.fori_loop(0, NODES_DEV // 16, combine, 0)
 
     row_t, lane_t = iota((COLS, COLS), 0), iota((COLS, COLS), 1)
     inner = jnp.where(

time: 97.7 us -> 93.6 us (0.958)
  Pallas kernels: 94 us -> 89.6 us
    pallas_call x1, Pallas kernels: 94 us -> 89.6 us  [shards(): pl.pallas_call(functools.partial(kernel, peers, slabs, cap), out_shape=(j...]
where the time goes in v7:
time: 93.6 us; the launch traced here: 93.1 us
  Pallas kernels  89.6 us (96%)
  local copies, waits for them, and re-layouts  2.84 us (3%)
    pallas_call x1, Pallas kernels, shards(): pl.pallas_call(functools.partial(kernel, peers, slabs, cap), out_shape=(j...  89.6 us
    unnamed x4, local copies, waits for them, and re-layouts  2.84 us

profile of v7, /device:TPU:5, one launch (start us, length us, event | category | flops | bytes accessed | tf_op | source)
XLA Modules:
  0.0 93.1 jit_solution(10689227198856836866)
XLA Ops:
  0.6 89.6 %shard_map.131 = (f32[1024,256]{1,0:T(8,128)}, f32[2,256]{1,0:T(2,128)}) custom-call(bf16[1024,256]{1,0:T(8,128)(2,1)} %probe_hbm.1, f32[8,128]{1,0:T(8,128)} %bitcast.5, f32[4]{0:T(128)} %theta_space_hbm.1, f32[4]{0:T(128)} %theta_time_hbm.1, bf16[8,128,128]{2,1,0:T(8,128)(2,1)} %diag_hbm.1, bf16[8,8,128,128]{3,2,1,0:T(8,128)(2,1)} %off_hbm.1, ...), custom_call_target="tpu_custom_call" | custom-call | tf_op jit(solution)/shard_map/pallas_call | solution.py:693
  90.2 0.0 copy-start
  90.2 2.3 %copy.16 = f32[1024,256]{1,0:T(8,128)} copy(f32[1024,256]{1,0:T(8,128)} %get-tuple-element.4) | data formatting | bytes 2097152
  92.5 0.0 copy-done
  92.5 0.6 copy.17
Async XLA Ops:
  90.2 2.3 %copy-start = (f32[2,256]{1,0:T(2,128)S(1)}, f32[2,256]{1,0:T(2,128)}, u32[]{:S(2)}) copy-start(f32[2,256]{1,0:T(2,128)} %get-tuple-element.5) | copy-start | bytes 6148
